TPU v7x, 128 devices: a whole 4x4x4 slice. The times are simulated.
128 devices in a mesh: lat: 8 (over z_lo, y), lon: 16 (over z_hi, x, core).
Axes of the slice: x: 4, y: 4, z: 4 (z_hi: 2, z_lo: 2; z = z_hi * 2 + z_lo), core: 2. Of those that a mesh axis runs over, the one named last changes fastest.
Arguments:
- latent: bfloat16 [2, 144, 384, 1024], P(None, 'lat', 'lon'), may hold values from -6 to 6
- grad_latent: bfloat16 [2, 144, 384, 1024], P(None, 'lat', 'lon'), may hold values from -6 to 6
- qkv_weight: bfloat16 [1024, 3072], replicated, may hold values from -0.1875 to 0.1875
- out_weight: bfloat16 [1024, 1024], replicated, may hold values from -0.1875 to 0.1875
- norm_gain: float32 [1024], replicated, may hold values from 0.25 to 1.75
- pair_bias: bfloat16 [16, 20736], replicated, may hold values from -4 to 390, as said below
Outputs:
- updated: bfloat16 [2, 144, 384, 1024], P(None, 'lat', 'lon')
- grad_input: bfloat16 [2, 144, 384, 1024], P(None, 'lat', 'lon')
- qkv_grad: float32 [1024, 3072], P(('lat', 'lon'))
- out_grad: float32 [1024, 1024], P(('lat', 'lon'))
Inputs may be any that keep to these rules, and one draw needn't show every extreme that they name: pair_bias[h, 144 a + b] is the bias of head h for query token a and key token b of a window.
All inputs are finite; a program needn't handle non-finite values.
Results may differ from a plain program's by a relative error of at most 0.013.
Values may be sent and summed in bfloat16 or wider, within the bound.
No kernel may reach another device: no remote copies, remote signals or barrier semaphores. Data moves between devices by JAX's collectives and lax.ppermute only.
A program may use at most 256 MiB of HBM per device.

v0:
```python
import jax
import jax.numpy as jnp
from jax import lax
from jax.sharding import PartitionSpec as P


def passed_along(value, axis, by):
    count = lax.axis_size(axis)
    return lax.ppermute(value, axis, [(i, (i + by) % count) for i in range(count)])


def to_windows(tile):
    levels, tile_rows, tile_cols, features = tile.shape
    split = tile.reshape(levels, tile_rows // 6, 6, tile_cols // 12, 12, features)
    return split.transpose(1, 3, 0, 2, 4, 5).reshape(-1, levels * 72, features)


def from_windows(flat, levels, tile_rows, tile_cols):
    features = flat.shape[-1]
    split = flat.reshape(tile_rows // 6, tile_cols // 12, levels, 6, 12, features)
    return split.transpose(2, 0, 3, 1, 4, 5).reshape(levels, tile_rows, tile_cols, features)


def block_pass(x_tile, g_tile, pole_rows, norm_gain, qkv_weight, out_weight, pair_bias):
    levels, tile_rows, tile_cols, features = x_tile.shape
    head_count = pair_bias.shape[0]
    head_size = features // head_count
    window_len = levels * 72
    score_scale = head_size ** (-0.5)
    token_win = to_windows(x_tile)
    grad_win = to_windows(g_tile)
    window_count = token_win.shape[0]
    f32 = jnp.float32
    bf16 = jnp.bfloat16
    as_float = token_win.astype(f32)
    average = jnp.mean(as_float, -1, keepdims=True)
    centred = as_float - average
    inv_std = lax.rsqrt(jnp.mean(centred * centred, -1, keepdims=True) + 1e-05)
    standard = centred * inv_std
    normed = (standard * norm_gain).astype(bf16).reshape(-1, features)
    projected = jnp.dot(normed, qkv_weight, preferred_element_type=f32).astype(bf16)
    projected = projected.reshape(window_count, window_len, 3, head_count, head_size)
    query_part = projected[:, :, 0]
    key_part = projected[:, :, 1]
    value_part = projected[:, :, 2]
    upper_half = jnp.arange(window_len) % 72 // 12 >= 3
    differ = upper_half[:, None] != upper_half[None, :]
    pole_win = jnp.repeat(pole_rows, tile_cols // 12)
    blocked = pole_win[:, None, None, None] & differ[None, None]
    pair_table = pair_bias.astype(f32).reshape(head_count, window_len, window_len)
    scores = (
        jnp.einsum("wqhd,wkhd->whqk", query_part, key_part, preferred_element_type=f32)
        * score_scale
        + pair_table[None]
    )
    scores = jnp.where(blocked, -1000000000.0, scores)
    peak_score = jnp.max(scores, -1, keepdims=True)
    exponent = jnp.exp(scores - peak_score)
    soft = exponent / jnp.sum(exponent, -1, keepdims=True)
    soft_b = soft.astype(bf16)
    attended = (
        jnp.einsum("whqk,wkhd->wqhd", soft_b, value_part, preferred_element_type=f32)
        .astype(bf16)
        .reshape(-1, features)
    )
    result = (
        as_float.reshape(-1, features) + jnp.dot(attended, out_weight, preferred_element_type=f32)
    ).astype(bf16)
    cotangent = grad_win.reshape(-1, features)
    term_output = jnp.einsum("ta,tb->ab", attended, cotangent, preferred_element_type=f32)
    grad_attended = jnp.einsum(
        "tb,ab->ta", cotangent, out_weight, preferred_element_type=f32
    ).astype(bf16)
    grad_attended = grad_attended.reshape(window_count, window_len, head_count, head_size)
    grad_soft = jnp.einsum("wqhd,wkhd->whqk", grad_attended, value_part, preferred_element_type=f32)
    inner_sum = jnp.sum(soft * grad_soft, -1, keepdims=True)
    grad_scores = (soft * (grad_soft - inner_sum) * score_scale).astype(bf16)
    grad_query = jnp.einsum(
        "whqk,wkhd->wqhd", grad_scores, key_part, preferred_element_type=f32
    ).astype(bf16)
    grad_key = jnp.einsum(
        "whqk,wqhd->wkhd", grad_scores, query_part, preferred_element_type=f32
    ).astype(bf16)
    grad_value = jnp.einsum(
        "whqk,wqhd->wkhd", soft_b, grad_attended, preferred_element_type=f32
    ).astype(bf16)
    grad_projected = jnp.stack([grad_query, grad_key, grad_value], 2).reshape(-1, 3 * features)
    term_proj = jnp.einsum("ta,tb->ab", normed, grad_projected, preferred_element_type=f32)
    grad_normed = jnp.einsum("tb,ab->ta", grad_projected, qkv_weight, preferred_element_type=f32)
    spread = grad_normed.reshape(window_count, window_len, features) * norm_gain
    grad_branch = inv_std * (
        spread
        - jnp.mean(spread, -1, keepdims=True)
        - standard * jnp.mean(spread * standard, -1, keepdims=True)
    )
    grad_total = (
        cotangent.astype(f32).reshape(window_count, window_len, features) + grad_branch
    ).astype(bf16)
    out_tile = from_windows(
        result.reshape(window_count, window_len, features), levels, tile_rows, tile_cols
    )
    grad_tile = from_windows(grad_total, levels, tile_rows, tile_cols)
    return (out_tile, grad_tile, term_proj, term_output)


def restore(tile):
    tile_rows = tile.shape[1]
    tile_cols = tile.shape[2]
    incoming = passed_along(tile[:, tile_rows - 3 :], "lat", 1)
    upright = jnp.concatenate([incoming, tile[:, : tile_rows - 3]], 1)
    beside = passed_along(upright[:, :, tile_cols - 6 :], "lon", 1)
    return jnp.concatenate([beside, upright[:, :, : tile_cols - 6]], 2)


def per_device(latent, grad_latent, qkv_weight, out_weight, norm_gain, pair_bias):
    levels, tile_rows, tile_cols, features = latent.shape
    lat_count = lax.axis_size("lat")
    lat_index = lax.axis_index("lat")
    edge_pair = passed_along(jnp.stack([latent[:, :, :6], grad_latent[:, :, :6]]), "lon", -1)
    wide_x = jnp.concatenate([latent, edge_pair[0]], 2)
    wide_g = jnp.concatenate([grad_latent, edge_pair[1]], 2)
    strip_send = jnp.stack([wide_x[:, :3], wide_g[:, :3]])
    strip_pair = passed_along(strip_send, "lat", -1)
    rolled_x = jnp.concatenate([wide_x[:, 3:], strip_pair[0]], 1)[:, :, 6:]
    rolled_g = jnp.concatenate([wide_g[:, 3:], strip_pair[1]], 1)[:, :, 6:]
    pole_rows = (jnp.arange(tile_rows // 6) == tile_rows // 6 - 1) & (lat_index == lat_count - 1)
    out_tile, grad_tile, term_proj, term_output = block_pass(
        rolled_x, rolled_g, pole_rows, norm_gain, qkv_weight, out_weight, pair_bias
    )
    updated = restore(out_tile)
    token_total = levels * tile_rows * tile_cols * lat_count * lax.axis_size("lon")
    factor = float(token_total) ** (-0.5)
    out_grad = (
        lax.psum_scatter(term_output, ("lat", "lon"), scatter_dimension=0, tiled=True) * factor
    )
    grad_input = restore(grad_tile)
    qkv_grad = lax.psum_scatter(term_proj, ("lat", "lon"), scatter_dimension=0, tiled=True)
    return (updated, grad_input, qkv_grad * factor, out_grad)


def solution(mesh):
    in_specs = (P(None, "lat", "lon", None), P(None, "lat", "lon", None), P(), P(), P(), P())
    out_specs = (
        P(None, "lat", "lon", None),
        P(None, "lat", "lon", None),
        P(("lat", "lon"), None),
        P(("lat", "lon"), None),
    )
    return jax.shard_map(
        per_device, mesh=mesh, in_specs=in_specs, out_specs=out_specs, check_vma=False
    )
```

profile of v0, /device:TPU:0, one launch (start us, length us, event | category | flops | bytes accessed | tf_op | source)
XLA Modules:
  0.0 1488.4 jit_solution(8962190236297356270)
XLA Ops:
  15.7 5.7 collective-permute-start
  21.5 4.4 reshape.204
  36.8 3.7 collective-permute-start.1
  43.0 10.7 collective-permute-done.1
  59.6 4.1 multiply_reduce_fusion.2
  67.0 5.4 pad_maximum_fusion.2
  73.0 5.4 copy.84
  80.5 3.8 reshape_reshape.7
  84.3 4.8 reshape.203
  89.2 10.9 convolution_convert_fusion
  100.1 13.8 reshape.195
  113.9 7.6 fusion.73
  121.5 6.5 copy.119
  128.0 6.5 copy.118
  134.5 6.5 copy.120
  141.0 10.9 fusion.74
  151.9 8.9 convert_bitcast_fusion.4
  160.8 6.7 copy.95
  167.4 5.9 reshape.196
  173.3 6.4 fusion.80
  179.8 3.9 multiply_convert_fusion.1
  185.7 3.9 convert_element_type.112
  189.6 4.7 convolution_convert_fusion.1
  194.3 5.8 reshape.199
  200.1 6.5 copy.100
  206.6 10.1 fusion.29
  216.7 24.3 %convert_bitcast_fusion.2 = bf16[6,144,1,16,64]{1,4,3,0,2:T(8,128)(2,1)} fusion(f32[6,16,144,144]{2,3,1,0:T(8,128)} %fusion.29, bf16[6,144,1,16,64]{1,4,3,0,2:T(8,128)(2,1)} %copy.119, f32[6,16,144,144]{2,3,1,0:T(8,128)} %get-tuple-element.26, f32[6,16,144]{2,1,0:T(8,128)S(1)} %get-tuple-element.25), kind=kOutput, calls=%fused_computation.42 | convolution fusion | flops 269637248 | bytes 19519488 | tf_op jit(solution)/shard_map/whqk,wqhd->wkhd/dot_general | solution.py:81
  241.0 24.7 %convert_bitcast_fusion.3 = bf16[6,144,1,16,64]{1,4,3,0,2:T(8,128)(2,1)} fusion(f32[6,16,144,144]{2,3,1,0:T(8,128)} %fusion.29, bf16[6,144,1,16,64]{1,4,3,0,2:T(8,128)(2,1)} %copy.120, f32[6,16,144,144]{2,3,1,0:T(8,128)} %get-tuple-element.26, f32[6,16,144]{2,1,0:T(8,128)S(1)} %get-tuple-element.25), kind=kOutput, calls=%fused_computation.43 | convolution fusion | flops 269637248 | bytes 19519488 | tf_op jit(solution)/shard_map/whqk,wkhd->wqhd/dot_general | solution.py:78
  265.7 10.3 convert_bitcast_fusion.1
  275.9 9.5 pad_maximum_fusion
  285.5 17.3 %copy.105 = bf16[6,144,3,16,64]{4,3,2,1,0:T(8,128)(2,1)} copy(bf16[6,144,3,16,64]{1,4,3,0,2:T(8,128)(2,1)} %pad_maximum_fusion) | data formatting | bytes 10616832 | tf_op jit(solution)/shard_map/stack | solution.py:87
  302.8 14.1 reshape.202
  316.9 11.9 fusion.79
  329.8 4.9 reshape.206
  334.7 14.1 dot_general.47
  348.8 5.8 add_convert_fusion.1
  354.6 3.9 reshape_reshape.6
  358.5 3.7 copy.96
  362.5 11.2 multiply_reduce_fusion.3
  378.9 4.8 reshape.205
  385.4 5.7 add_convert_fusion
  391.0 3.9 reshape.200
  401.3 9.2 collective-permute-done.4
  411.2 3.8 fusion.49
  416.7 6.0 collective-permute-done.5
  422.7 3.7 fusion.48
  428.1 397.5 %reduce-scatter.5.cloned.1.call-done = f32[8,1024]{1,0:T(8,128)} async-done(((f32[1024,1024]{1,0:T(8,128)}), f32[8,1024]{1,0:T(8,128)}) %reduce-scatter.5.cloned.1.call-update) | async-done | bytes 32784 | tf_op jit(solution)/shard_map/reduce_scatter | solution.py:134
  827.0 652.8 %reduce-scatter.3.cloned.1.call-done = f32[8,3072]{1,0:T(8,128)} async-done(((f32[1024,3072]{1,0:T(8,128)}), f32[8,3072]{1,0:T(8,128)}) %reduce-scatter.3.cloned.1.call-update) | async-done | bytes 98320 | tf_op jit(solution)/shard_map/reduce_scatter | solution.py:137
  (93 shorter events, 57.3 us)
Async XLA Ops:
  7.2 182.4 %copy-start = (bf16[1024,1024]{1,0:T(8,128)(2,1)S(1)}, bf16[1024,1024]{1,0:T(8,128)(2,1)}, u32[]{:S(2)}) copy-start(bf16[1024,1024]{1,0:T(8,128)(2,1)} %param.9) | copy-start | bytes 6291460
  7.2 818.4 %reduce-scatter.5.cloned.1.call-start = ((), (), s32[]{:S(2)}) async-start(), calls=%async_computation.3 | async-start | bytes 4227072 | tf_op jit(solution)/shard_map/reduce_scatter | solution.py:134
  7.2 3.5 copy-start.12
  10.7 5.0 copy-start.6
  12.5 1.2 copy-start.3
  15.7 16.2 %collective-permute-start = (bf16[2,2,18,6,1024]{4,1,3,2,0:T(2,128)(2,1)S(1)}, bf16[2,2,18,6,1024]{4,1,3,2,0:T(2,128)(2,1)}, u32[]{:S(2)}, u32[]{:S(2)}) collective-permute-start(bf16[2,2,18,6,1024]{4,1,3,2,0:T(2,128)(2,1)S(1)} %pad_maximum_fusion.6), channel_id=1, source_target_pairs={{0,15},{1,0},{2,1},{3,2},{4,3},{5,4},{6,5},{7,6},{8,7},{9,8},{10,9... | collective-permute-start | bytes 2654216 | tf_op jit(solution)/shard_map/ppermute | solution.py:9
  29.4 5.9 copy-start.4
  33.7 6.9 copy-start.7
  36.8 16.9 %collective-permute-start.1 = (bf16[2,2,3,30,1024]{4,1,3,2,0:T(2,128)(2,1)S(1)}, bf16[2,2,3,30,1024]{4,1,3,2,0:T(2,128)(2,1)S(1)}, u32[]{:S(2)}, u32[]{:S(2)}) collective-permute-start(bf16[2,2,3,30,1024]{4,1,3,2,0:T(2,128)(2,1)S(1)} %pad_maximum_fusion.7), channel_id=1, source_target_pairs={{0,112},{16,0},{32,16},{48,32},{64,48},{80,64},{96,80},{112,96},{1... | collective-permute-start | bytes 2211848 | tf_op jit(solution)/shard_map/ppermute | solution.py:9
  56.5 1.2 copy-start.1
  59.6 12.8 copy-start.13
  59.6 4.1 copy-start.2
  59.6 7.4 copy-start.5
  72.9 5.5 copy-start.15
  73.0 5.4 copy-start.8
  84.3 4.8 copy-start.18
  134.5 6.5 copy-start.17
  179.8 1300.0 %reduce-scatter.3.cloned.1.call-start = ((), (), s32[]{:S(2)}) async-start(), calls=%async_computation.2 | async-start | bytes 12681216 | tf_op jit(solution)/shard_map/reduce_scatter | solution.py:137
  328.8 0.8 copy-start.14
  328.9 0.9 copy-start.16
  358.5 4.0 copy-start.10
  362.4 11.3 copy-start.9
  362.4 21.3 %collective-permute-start.2 = (bf16[2,3,24,1024]{3,0,2,1:T(2,128)(2,1)S(1)}, bf16[2,3,24,1024]{3,0,2,1:T(2,128)(2,1)S(1)}, u32[]{:S(2)}, u32[]{:S(2)}) collective-permute-start(bf16[2,3,24,1024]{3,0,2,1:T(2,128)(2,1)S(1)} %slice.102), channel_id=1, source_target_pairs={{0,16},{16,32},{32,48},{48,64},{64,80},{80,96},{96,112},{112,0},{1... | collective-permute-start | bytes 884744 | tf_op jit(solution)/shard_map/ppermute | solution.py:9
  385.3 25.9 %collective-permute-start.3 = (bf16[2,18,6,1024]{3,0,2,1:T(2,128)(2,1)S(1)}, bf16[2,18,6,1024]{3,0,2,1:T(2,128)(2,1)S(1)}, u32[]{:S(2)}, u32[]{:S(2)}) collective-permute-start(bf16[2,18,6,1024]{3,0,2,1:T(2,128)(2,1)S(1)} %pad_maximum_fusion.9), channel_id=1, source_target_pairs={{0,1},{1,2},{2,3},{3,4},{4,5},{5,6},{6,7},{7,8},{8,9},{9,10},{10,1... | collective-permute-start | bytes 1327112 | tf_op jit(solution)/shard_map/ppermute | solution.py:9
  398.4 12.8 copy-start.11
  398.6 11.9 collective-permute-start.4
  411.1 11.6 collective-permute-start.5
Sparse Core Ops, SparseCore 0:
  179.9 645.6 reduce-scatter.4
  828.1 651.6 reduce-scatter.2
where the time goes:
time: 1500 us; the launch traced here: 1490 us
  waiting for transfers between devices  1080 us (72%)
  local copies, waits for them, and re-layouts  189 us (13%)
  matrix products  140 us (9%)
  other arithmetic  55.9 us (4%)
    reduce_scatter x1, waiting for transfers between devices, per_device(): lax.psum_scatter(term_proj, ('lat', 'lon'), scatter_dimension=0, tiled=True)  653 us
    reduce_scatter x1, waiting for transfers between devices, per_device(): lax.psum_scatter(term_output, ('lat', 'lon'), scatter_dimension=0, tiled=...  397 us
    unnamed x45, local copies, waits for them, and re-layouts  31.5 us
  transfers between devices with their start and end apart: 8, of which 6 were waited for; matrix products, arithmetic and copies ran while one was open for 16% of the time, Pallas kernels for 0%

commit v1 on v0

v1 whole, which is shorter than its diff:
```python
import jax
import jax.numpy as jnp
from jax import lax
from jax.experimental import pallas as pl
from jax.experimental.pallas import tpu as pltpu
from jax.sharding import PartitionSpec as P

f32 = jnp.float32
bf16 = jnp.bfloat16
D = 1024
HEADS = 16
QUADS = 4
QW = 256
WIN = 144
TOK = 864
LANES = 4 * WIN
BLOCKED = -1e9
VMEM_LIMIT = 56 * 1024 * 1024
EPS = 1e-05


def nt(a, b):
    return lax.dot_general(a, b, (((1,), (1,)), ((), ())), preferred_element_type=f32)


def tn(a, b):
    return lax.dot_general(a, b, (((0,), (0,)), ((), ())), preferred_element_type=f32)


def nn(a, b):
    return jnp.dot(a, b, preferred_element_type=f32)


def index_of(x, y, z, c):
    return ((z % 2) * 4 + y) * 16 + (z // 2) * 8 + x * 2 + c


def place_of(index):
    lat, lon = index // 16, index % 16
    return dict(x=(lon // 2) % 4, y=lat % 4, z=(lon // 8) * 2 + lat // 4, c=lon % 2)


def my_place(axis):
    lat, lon = lax.axis_index("lat"), lax.axis_index("lon")
    return dict(x=(lon // 2) % 4, y=lat % 4, z=(lon // 8) * 2 + lat // 4, c=lon % 2)[axis]


def shift(value, axis, by):
    size = 2 if axis == "c" else 4
    pairs = []
    for src in range(128):
        place = place_of(src)
        place[axis] = (place[axis] + by) % size
        pairs.append((src, index_of(**place)))
    return lax.ppermute(value, ("lat", "lon"), pairs)


def shift_grid(value, dlat, dlon):
    pairs = []
    for lat in range(8):
        for lon in range(16):
            pairs.append((lat * 16 + lon, ((lat + dlat) % 8) * 16 + (lon + dlon) % 16))
    return lax.ppermute(value, ("lat", "lon"), pairs)


def row_order(axes):
    order = []
    for c in range(2):
        for i in range(4):
            for j in range(4):
                for k in range(4):
                    place = dict(zip(axes, (i, j, k)))
                    order.append(index_of(c=c, **place))
    return order


def ordered_rows(value, order):
    return jnp.concatenate([value[8 * p : 8 * p + 8] for p in order], 0)


def prologue_kernel(lat_ref, grad_ref, cols_ref, rows_ref, corner_ref, gain_ref, xw_ref, gw_ref, nt_ref, n_ref, xs, gs):
    for which, (tile, store) in enumerate(((lat_ref, xs), (grad_ref, gs))):
        for l in range(2):
            for i in range(18):
                if i < 15:
                    main = tile[l, i + 3].astype(f32)
                    side = cols_ref[which, l, i + 3].astype(f32)
                else:
                    main = rows_ref[which, l, i - 15].astype(f32)
                    side = corner_ref[which, l, i - 15].astype(f32)
                left = (i // 6) * 2 * WIN + l * 72 + (i % 6) * 12
                right = left + WIN
                store[left : left + 12] = main[6:18]
                store[right : right + 6] = main[18:24]
                store[right + 6 : right + 12] = side
    order = row_order("xyz")
    gain = gain_ref[...]

    for w in range(6):
        rows = pl.ds(w * WIN, WIN)
        x = xs[rows]
        centred = x - jnp.mean(x, -1, keepdims=True)
        inv_std = lax.rsqrt(jnp.mean(centred * centred, -1, keepdims=True) + EPS)
        normed = centred * inv_std * gain
        n_ref[rows] = normed.astype(bf16)
        xw_ref[rows] = x.astype(bf16)
        gw_ref[rows] = gs[rows].astype(bf16)
    for half in range(4):
        block = n_ref[:, half * QW : (half + 1) * QW].astype(f32)
        nt_ref[half * QW : (half + 1) * QW] = block.T.astype(bf16)


def prologue(latent, grad_latent, cols, rows, corner, gain):
    return pl.pallas_call(
        prologue_kernel,
        out_shape=(
            jax.ShapeDtypeStruct((TOK, D), bf16),
            jax.ShapeDtypeStruct((TOK, D), bf16),
            jax.ShapeDtypeStruct((D, TOK), bf16),
            jax.ShapeDtypeStruct((TOK, D), bf16),
        ),
        scratch_shapes=[pltpu.VMEM((TOK, D), f32), pltpu.VMEM((TOK, D), f32)],
        compiler_params=pltpu.CompilerParams(vmem_limit_bytes=VMEM_LIMIT),
        name="prologue",
    )(latent, grad_latent, cols, rows, corner, gain)


def quad_kernel(
    pole_ref, n_ref, nt_ref, gw_ref, wq_ref, wk_ref, wv_ref, wo_ref, bias_ref,
    att_ref, gp_ref, grad_ref, q, k, v, da,
):
    n = n_ref[...]
    q[...] = nn(n, wq_ref[...]).astype(bf16)
    k[...] = nn(n, wk_ref[...]).astype(bf16)
    v[...] = nn(n, wv_ref[...]).astype(bf16)
    da[...] = nt(gw_ref[...], wo_ref[...]).astype(bf16)
    lane_head = lax.broadcasted_iota(jnp.int32, (WIN, QW), 1) // 64

    def apart(value):
        zero = jnp.zeros_like(value)
        return jnp.concatenate([jnp.where(lane_head == h, value, zero) for h in range(4)], 0)

    def gathered(stacked):
        out = stacked[:WIN]
        for h in range(1, 4):
            out = jnp.where(lane_head == h, stacked[h * WIN : (h + 1) * WIN], out)
        return out

    def window(w, carry):
        rows = pl.ds(pl.multiple_of(w * WIN, WIN), WIN)
        variant = jnp.where(w >= 4, pole_ref[0], 0)
        qw, kw, vw, dw = q[rows], k[rows], v[rows], da[rows]
        q_apart = apart(qw * jnp.asarray(0.125, bf16))
        d_apart = apart(dw)
        s = nt(kw, q_apart) + bias_ref[variant, 0].astype(f32)
        e = jnp.exp(s - jnp.max(s, 0, keepdims=True))
        soft = e * (1.0 / jnp.sum(e, 0, keepdims=True))
        soft_b = soft.astype(bf16)
        att_ref[rows] = gathered(tn(soft_b, vw)).astype(bf16)
        dv = nn(soft_b, d_apart)
        dp = nt(vw, d_apart)
        inner = jnp.sum(soft * dp, 0, keepdims=True)
        ds = (soft * (dp - inner)).astype(bf16)
        dk = nn(ds, q_apart)
        dq = gathered(tn(ds, kw)) * 0.125
        gp_ref[0, rows] = dq.astype(bf16)
        gp_ref[1, rows] = dk.astype(bf16)
        gp_ref[2, rows] = dv.astype(bf16)
        return carry

    lax.fori_loop(0, 6, window, 0)
    order = row_order("xyz")
    for part in range(3):
        grad_ref[:, part] = ordered_rows(nn(nt_ref[...], gp_ref[part]), order).astype(bf16).reshape(2, 512, QW)


def quads(pole, normed, normed_t, gw, qkv_weight, out_weight, bias, first, count):
    def whole(shape):
        return pl.BlockSpec(shape, lambda g, pole: (0,) * len(shape))

    def columns(part):
        return pl.BlockSpec((D, QW), lambda g, pole: (0, part * QUADS + first + g))

    return pl.pallas_call(
        quad_kernel,
        grid_spec=pltpu.PrefetchScalarGridSpec(
            num_scalar_prefetch=1,
            grid=(count,),
            in_specs=[
                whole((TOK, D)), whole((D, TOK)), whole((TOK, D)),
                columns(0), columns(1), columns(2),
                pl.BlockSpec((QW, D), lambda g, pole: (first + g, 0)),
                pl.BlockSpec((2, 1, WIN, LANES), lambda g, pole: (0, first + g, 0, 0)),
            ],
            out_specs=[
                pl.BlockSpec((TOK, QW), lambda g, pole: (0, g)),
                pl.BlockSpec((3, TOK, QW), lambda g, pole: (0, 0, g)),
                pl.BlockSpec((2, 3, 512, QW), lambda g, pole: (0, 0, 0, g)),
            ],
            scratch_shapes=[pltpu.VMEM((TOK, QW), bf16)] * 4,
        ),
        out_shape=(
            jax.ShapeDtypeStruct((TOK, count * QW), bf16),
            jax.ShapeDtypeStruct((3, TOK, count * QW), bf16),
            jax.ShapeDtypeStruct((2, 3, 512, count * QW), bf16),
        ),
        compiler_params=pltpu.CompilerParams(vmem_limit_bytes=VMEM_LIMIT),
        name="quads",
    )(pole, normed, normed_t, gw, qkv_weight, qkv_weight, qkv_weight, out_weight, bias)


def out_grad_kernel(att_ref, gw_ref, grad_ref):
    order = row_order("xyz")
    att = att_ref[...].astype(f32).T.astype(bf16)
    grad_ref[...] = ordered_rows(nn(att, gw_ref[...]), order).astype(bf16).reshape(2, 512, QW)


def out_grads(att, gw):
    return pl.pallas_call(
        out_grad_kernel,
        grid=(QUADS,),
        in_specs=[pl.BlockSpec((TOK, D), lambda n: (0, 0)), pl.BlockSpec((TOK, QW), lambda n: (0, n))],
        out_specs=pl.BlockSpec((2, 512, QW), lambda n: (0, 0, n)),
        out_shape=jax.ShapeDtypeStruct((2, 512, D), bf16),
        compiler_params=pltpu.CompilerParams(vmem_limit_bytes=VMEM_LIMIT),
        name="out_grads",
    )(att, gw)


def epilogue_kernel(att_ref, gp_ref, wo_ref, w_ref, xw_ref, gw_ref, gain_ref, out_ref, grad_ref, so, sg):
    x = xw_ref[...].astype(f32)
    so[...] = x + nn(att_ref[...], wo_ref[...])
    gn = nt(gp_ref[0], w_ref[:, :D]) + nt(gp_ref[1], w_ref[:, D : 2 * D]) + nt(gp_ref[2], w_ref[:, 2 * D :])
    centred = x - jnp.mean(x, -1, keepdims=True)
    inv_std = lax.rsqrt(jnp.mean(centred * centred, -1, keepdims=True) + EPS)
    unit = centred * inv_std
    e = gn * gain_ref[...]
    branch = inv_std * (e - jnp.mean(e, -1, keepdims=True) - unit * jnp.mean(e * unit, -1, keepdims=True))
    sg[...] = gw_ref[...].astype(f32) + branch
    for l in range(2):
        for r in range(6):
            at = l * 72 + r * 12
            for src, dst in ((so, out_ref), (sg, grad_ref)):
                line = jnp.concatenate([src[at : at + 12], src[WIN + at : WIN + at + 12]], 0)
                dst[l, r] = line.astype(bf16)


def epilogue(att, gp, out_weight, qkv_weight, xw, gw, gain):
    rows = 2 * WIN
    tile = pl.BlockSpec((2, 6, 24, D), lambda i: (0, i, 0, 0))
    return pl.pallas_call(
        epilogue_kernel,
        grid=(3,),
        in_specs=[
            pl.BlockSpec((rows, D), lambda i: (i, 0)),
            pl.BlockSpec((3, rows, D), lambda i: (0, i, 0)),
            pl.BlockSpec((D, D), lambda i: (0, 0)),
            pl.BlockSpec((D, 3 * D), lambda i: (0, 0)),
            pl.BlockSpec((rows, D), lambda i: (i, 0)),
            pl.BlockSpec((rows, D), lambda i: (i, 0)),
            pl.BlockSpec((1, D), lambda i: (0, 0)),
        ],
        out_specs=[tile, tile],
        out_shape=[jax.ShapeDtypeStruct((2, 18, 24, D), bf16)] * 2,
        scratch_shapes=[pltpu.VMEM((rows, D), f32)] * 2,
        compiler_params=pltpu.CompilerParams(vmem_limit_bytes=VMEM_LIMIT),
        name="epilogue",
    )(att, gp, out_weight, qkv_weight, xw, gw, gain)


def restore_kernel(out_ref, grad_ref, cols_ref, rows_ref, corner_ref, updated_ref, back_ref):
    for which, (src, dst) in enumerate(((out_ref, updated_ref), (grad_ref, back_ref))):
        for l in range(2):
            for i in range(18):
                if i < 3:
                    main = rows_ref[which, l, i].astype(f32)
                    side = corner_ref[which, l, i].astype(f32)
                else:
                    main = src[l, i - 3].astype(f32)
                    side = cols_ref[which, l, i - 3].astype(f32)
                dst[l, i] = jnp.concatenate([side, main[:18]], 0).astype(bf16)


def restored(out, grad, cols, rows, corner):
    return pl.pallas_call(
        restore_kernel,
        out_shape=[jax.ShapeDtypeStruct((2, 18, 24, D), bf16)] * 2,
        compiler_params=pltpu.CompilerParams(vmem_limit_bytes=VMEM_LIMIT),
        name="restore",
    )(out, grad, cols, rows, corner)


def pick(v, i):
    return lax.dynamic_index_in_dim(v, i, 0, keepdims=False)


def core_stage(v):
    m = my_place("c")
    r = shift(pick(v, 1 - m), "c", 1)
    return (pick(v, m).astype(f32) + r.astype(f32)).astype(bf16)


def ring_stage(v, axis):
    m = my_place(axis)
    up = shift(pick(v, (m + 1) % 4), axis, 1)
    down = shift(pick(v, (m + 3) % 4), axis, -1)
    far = shift(pick(v, (m + 2) % 4), axis, 2)
    return pick(v, m).astype(f32) + up.astype(f32) + down.astype(f32) + far.astype(f32)


def reduce_scatter(v, order):
    v = core_stage(v)
    for i, axis in enumerate(order):
        v = ring_stage(v.reshape(4, -1, v.shape[-1]), axis)
        if i < 2:
            v = v.astype(bf16)
    return v


def per_device(latent, grad_latent, qkv_weight, out_weight, norm_gain, pair_bias):
    both = jnp.stack([latent, grad_latent])
    cols = shift_grid(both[:, :, :, :6], 0, -1)
    rows = shift_grid(both[:, :, :3], -1, 0)
    corner = shift_grid(both[:, :, :3, :6], -1, -1)
    gain = norm_gain.reshape(1, D)

    table = pair_bias.reshape(QUADS, 4, WIN, WIN).transpose(0, 3, 1, 2)
    upper = jnp.arange(WIN) % 72 // 12 >= 3
    differ = upper[:, None, None] != upper[None, None, :]
    bias = jnp.stack([table, jnp.where(differ, jnp.asarray(BLOCKED, bf16), table)])
    bias = bias.reshape(2, QUADS, WIN, LANES)
    pole = (lax.axis_index("lat") == lax.axis_size("lat") - 1).astype(jnp.int32).reshape(1)

    xw, gw, normed_t, normed = prologue(latent, grad_latent, cols, rows, corner, gain)
    att, gp, qkv_part = quads(pole, normed, normed_t, gw, qkv_weight, out_weight, bias, 0, QUADS)
    out_part = out_grads(att, gw)
    out_tile, grad_tile = epilogue(att, gp, out_weight, qkv_weight, xw, gw, gain)
    tiles = jnp.stack([out_tile, grad_tile])
    cols = shift_grid(tiles[:, :, :15, 18:], 0, 1)
    rows = shift_grid(tiles[:, :, 15:], 1, 0)
    corner = shift_grid(tiles[:, :, 15:, 18:], 1, 1)
    updated, grad_input = restored(out_tile, grad_tile, cols, rows, corner)

    factor = 110592.0 ** (-0.5)
    part = jnp.concatenate([qkv_part, out_part[:, None]], 1)
    part = part.transpose(0, 2, 1, 3).reshape(2, 512, 4 * D)
    grads = reduce_scatter(part, "xyz") * factor
    return (updated, grad_input, grads[:, : 3 * D], grads[:, 3 * D :])


def solution(mesh):
    in_specs = (P(None, "lat", "lon", None), P(None, "lat", "lon", None), P(), P(), P(), P())
    out_specs = (
        P(None, "lat", "lon", None),
        P(None, "lat", "lon", None),
        P(("lat", "lon"), None),
        P(("lat", "lon"), None),
    )
    return jax.shard_map(
        per_device, mesh=mesh, in_specs=in_specs, out_specs=out_specs, check_vma=False
    )
```

time: 1500 us -> 235 us (0.16)
  waiting for transfers between devices: 1080 us -> 57.5 us
  local copies, waits for them, and re-layouts: 189 us -> 38.8 us
  matrix products: 140 us -> 0 us
  Pallas kernels: 0 us -> 78 us
  other arithmetic: 55.9 us -> 21.7 us
  starting transfers between devices: 11.1 us -> 33.4 us
    reduce_scatter x2 -> x0, waiting for transfers between devices: 1050 us -> none  [the longest x1 653 us: per_device(): lax.psum_scatter(term_proj, ('lat', 'lon'), scatter_dimension=0, tiled=True)]
    dot_general x11 -> x0, matrix products: 129 us -> none  [the longest x1 24.7 us: block_pass(): jnp.einsum('whqk,wkhd->wqhd', grad_scores, key_part, preferred_element_ty...]
    pallas_call x0 -> x5, Pallas kernels: none -> 78 us  [the longest x1 45 us: quads(): pl.pallas_call(quad_kernel, grid_spec=pltpu.PrefetchScalarGridSpec(num_sc...]
    reshape x6 -> x3, local copies, waits for them, and re-layouts: 50 us -> 9.82 us  [the longest x1 6.39 us: reduce_scatter(): v = ring_stage(v.reshape(4, -1, v.shape[-1]), axis)]
    convert_element_type x8 -> x0, local copies, waits for them, and re-layouts: 35.3 us -> none  [the longest x3 15.1 us: block_pass(): as_float = token_win.astype(f32)]
    unnamed x45 -> x16, local copies, waits for them, and re-layouts: 31.5 us -> 0.89 us
    ppermute x6 -> x16, waiting for transfers between devices: 27.5 us -> 57.5 us  [the longest x10 46.5 us: shift(): return lax.ppermute(value, ('lat', 'lon'), pairs)]
    another operation x4 -> x2, local copies, waits for them, and re-layouts: 25.7 us -> 1.53 us  [per_device(): jnp.stack([table, jnp.where(differ, jnp.asarray(BLOCKED, bf16), table)])]
  transfers between devices with their start and end apart: 8 -> 16, of which waited for: 6 -> 9; matrix products, arithmetic and copies ran while one was open for 16% -> 6% of each run, Pallas kernels for 0% -> 9%
where the time goes in v1:
time: 235 us; the launch traced here: 230 us
  Pallas kernels  78 us (33%)
  waiting for transfers between devices  57.5 us (24%)
  local copies, waits for them, and re-layouts  38.8 us (17%)
  starting transfers between devices  33.4 us (14%)
  other arithmetic  21.7 us (9%)
    ppermute x10, waiting for transfers between devices, shift(): return lax.ppermute(value, ('lat', 'lon'), pairs)  46.5 us
    pallas_call x1, Pallas kernels, quads(): pl.pallas_call(quad_kernel, grid_spec=pltpu.PrefetchScalarGridSpec(num_sc...  45 us
    ppermute x10, starting transfers between devices, shift(): return lax.ppermute(value, ('lat', 'lon'), pairs)  21.8 us
    pallas_call x1, Pallas kernels, epilogue(): pl.pallas_call(epilogue_kernel, grid=(3,), in_specs=[pl.BlockSpec((rows,...  15.1 us
    ppermute x6, starting transfers between devices, shift_grid(): return lax.ppermute(value, ('lat', 'lon'), pairs)  11.6 us
    transpose x1, local copies, waits for them, and re-layouts, per_device(): part = part.transpose(0, 2, 1, 3).reshape(2, 512, 4 * D)  11.5 us
    ppermute x6, waiting for transfers between devices, shift_grid(): return lax.ppermute(value, ('lat', 'lon'), pairs)  11 us
    squeeze x4, local copies, waits for them, and re-layouts, pick(): return lax.dynamic_index_in_dim(v, i, 0, keepdims=False)  7.57 us
  transfers between devices with their start and end apart: 16, of which 9 were waited for; matrix products, arithmetic and copies ran while one was open for 6% of the time, Pallas kernels for 9%

profile of v1, /device:TPU:0, one launch (start us, length us, event | category | flops | bytes accessed | tf_op | source)
XLA Modules:
  0.0 230.3 jit_solution(15912327915854648373)
XLA Ops:
  0.6 1.5 fusion.4
  2.1 1.8 copy.26
  4.0 5.6 %collective-permute-start = (bf16[2,2,18,6,1024]{4,1,3,2,0:T(2,128)(2,1)}, bf16[2,2,18,6,1024]{4,1,3,2,0:T(2,128)(2,1)}, u32[]{:S(2)}, u32[]{:S(2)}) collective-permute-start(bf16[2,2,18,6,1024]{4,1,3,2,0:T(2,128)(2,1)} %copy.26), channel_id=1, source_target_pairs={{0,15},{1,0},{2,1},{3,2},{4,3},{5,4},{6,5},{7,6},{8,7},{9,8},{10,9... | collective-permute-start | bytes 2654216 | tf_op jit(solution)/shard_map/ppermute | solution.py:63
  9.6 0.9 fusion.5
  10.4 3.5 %collective-permute-start.1 = (bf16[2,2,3,24,1024]{4,3,2,1,0:T(8,128)(2,1)}, bf16[2,2,3,24,1024]{4,3,2,1,0:T(8,128)(2,1)}, u32[]{:S(2)}, u32[]{:S(2)}) collective-permute-start(bf16[2,2,3,24,1024]{4,3,2,1,0:T(8,128)(2,1)} %fusion.5), channel_id=1, source_target_pairs={{0,112},{1,113},{2,114},{3,115},{4,116},{5,117},{6,118},{7,119},{8... | collective-permute-start | bytes 1769480 | tf_op jit(solution)/shard_map/ppermute | solution.py:63
  13.9 0.3 collective-permute-start.2
  14.3 2.1 reshape.101
  16.4 1.3 copy.28
  17.8 0.7 broadcast_select_fusion
  18.6 0.8 stack.31
  19.4 0.8 stack.30
  20.2 1.3 pad_maximum_fusion.bias_ref
  21.5 2.5 %copy.27.cols_ref = bf16[2,2,18,6,1024]{4,3,2,1,0:T(8,128)(2,1)} copy(bf16[2,2,18,6,1024]{4,1,3,2,0:T(2,128)(2,1)} %collective-permute-done) | data formatting | bytes 1769472 | tf_op jit(solution)/shard_map/ppermute | solution.py:63
  24.0 3.1 %collective-permute-done.1.rows_ref = bf16[2,2,3,24,1024]{4,3,2,1,0:T(8,128)(2,1)} collective-permute-done((bf16[2,2,3,24,1024]{4,3,2,1,0:T(8,128)(2,1)}, bf16[2,2,3,24,1024]{4,3,2,1,0:T(8,128)(2,1)}, u32[]{:S(2)}, u32[]{:S(2)}) %collective-permute-start.1) | collective-permute-done | bytes 589856 | tf_op jit(solution)/shard_map/ppermute | solution.py:63
  27.1 6.8 %prologue.1 = (bf16[864,1024]{1,0:T(8,128)(2,1)}, bf16[864,1024]{1,0:T(8,128)(2,1)}, bf16[1024,864]{1,0:T(8,128)(2,1)}, bf16[864,1024]{1,0:T(8,128)(2,1)}) custom-call(bf16[2,18,24,1024]{3,2,1,0:T(8,128)(2,1)} %lat_ref.1, bf16[2,18,24,1024]{3,2,1,0:T(8,128)(2,1)} %grad_ref.1, bf16[2,2,18,6,1024]{4,3,2,1,0:T(8,128)(2,1)} %copy.27.cols_ref, ...), custom_call_target="tpu_custom_call" | custom-call | tf_op jit(solution)/shard_map/prologue/pallas_call | solution.py:114
  33.9 45.0 %quads.1 = (bf16[864,1024]{1,0:T(8,128)(2,1)}, bf16[3,864,1024]{2,1,0:T(8,128)(2,1)}, bf16[2,3,512,1024]{3,2,1,0:T(8,128)(2,1)}) custom-call(s32[1]{0:T(128)} %bitcast.pole_ref, bf16[864,1024]{1,0:T(8,128)(2,1)} %get-tuple-element.15.n_ref, bf16[1024,864]{1,0:T(8,128)(2,1)} %get-tuple-element.16.nt_ref, bf16[864,1024]{1,0:T(8,128)(2,1)} %get-tuple-element.17.gw_ref, ...), custom_call_target="tpu_custom_call" | custom-call | tf_op jit(solution)/shard_map/quads/pallas_call | solution.py:184
  78.9 6.4 %out_grads.1 = bf16[2,512,1024]{2,1,0:T(8,128)(2,1)} custom-call(bf16[864,1024]{1,0:T(8,128)(2,1)} %get-tuple-element.18.att_ref, bf16[864,1024]{1,0:T(8,128)(2,1)} %get-tuple-element.17.gw_ref), custom_call_target="tpu_custom_call" | custom-call | tf_op jit(solution)/shard_map/out_grads/pallas_call | solution.py:219
  85.3 7.4 %maximum_bitcast_fusion = bf16[2,512,4,1024]{3,1,2,0:T(8,128)(2,1)} fusion(bf16[2,1,512,1024]{3,2,1,0:T(8,128)(2,1)} %bitcast.67, bf16[2,3,512,1024]{3,2,1,0:T(8,128)(2,1)} %get-tuple-element.25), kind=kLoop, calls=%fused_computation | loop fusion | flops 4194304 | bytes 16777216 | tf_op jit(solution)/shard_map/transpose | solution.py:346
  92.7 11.5 %copy.32 = bf16[2,512,4,1024]{1,3,2,0:T(8,128)(2,1)} copy(bf16[2,512,4,1024]{3,1,2,0:T(8,128)(2,1)} %maximum_bitcast_fusion) | data formatting | bytes 16777216 | tf_op jit(solution)/shard_map/transpose | solution.py:346
  104.1 4.4 %dynamic-slice_bitcast_fusion = bf16[512,4096]{0,1:T(8,128)(2,1)} fusion(bf16[2,512,4096]{1,2,0:T(8,128)(2,1)} %bitcast.50, s32[]{:T(128)S(6)} %select_n.143), kind=kLoop, calls=%fused_computation.3 | loop fusion | bytes 8388612 | tf_op jit(solution)/shard_map/jit(dynamic_index_in_dim)/squeeze | solution.py:294
  108.6 7.5 %collective-permute-done.6 = bf16[512,4096]{0,1:T(8,128)(2,1)} collective-permute-done((bf16[512,4096]{0,1:T(8,128)(2,1)}, bf16[512,4096]{0,1:T(8,128)(2,1)}, u32[]{:S(2)}, u32[]{:S(2)}) %collective-permute-start.6) | collective-permute-done | bytes 4194336 | tf_op jit(solution)/shard_map/ppermute | solution.py:55
  116.1 6.6 %fusion = bf16[512,4096]{0,1:T(8,128)(2,1)} fusion(bf16[512,4096]{0,1:T(8,128)(2,1)} %collective-permute-done.6, bf16[2,512,4096]{1,2,0:T(8,128)(2,1)} %bitcast.51, s32[]{:T(128)S(6)} %select_n.142), kind=kLoop, calls=%fused_computation.2 | loop fusion | flops 8388608 | bytes 12582916 | tf_op jit(solution)/shard_map/convert_element_type | solution.py:300
  122.7 6.4 %copy.37 = bf16[512,4096]{1,0:T(8,128)(2,1)} copy(bf16[512,4096]{0,1:T(8,128)(2,1)} %fusion) | data formatting | bytes 8388608 | tf_op jit(solution)/shard_map/reshape | solution.py:314
  129.1 3.1 %dynamic-slice_bitcast_fusion.3 = (bf16[128,4096]{1,0:T(8,128)(2,1)S(1)}, bf16[128,4096]{1,0:T(8,128)(2,1)}, bf16[128,4096]{1,0:T(8,128)(2,1)S(1)}) fusion(bf16[4,128,4096]{2,1,0:T(8,128)(2,1)} %bitcast.64, s32[]{:T(128)S(6)} %select_n.148, s32[]{:T(128)S(6)} %select_n.152, s32[]{:T(128)S(6)} %select_n.150), kind=kLoop, calls=%fused_computation.17 | loop fusion | bytes 6291468 | tf_op jit(solution)/shard_map/jit(dynamic_index_in_dim)/squeeze | solution.py:294
  132.1 3.4 %collective-permute-start.9 = (bf16[128,4096]{1,0:T(8,128)(2,1)}, bf16[128,4096]{1,0:T(8,128)(2,1)S(1)}, u32[]{:S(2)}, u32[]{:S(2)}) collective-permute-start(bf16[128,4096]{1,0:T(8,128)(2,1)} %get-tuple-element.27), channel_id=1, source_target_pairs={{0,4},{1,5},{2,6},{3,7},{4,0},{5,1},{6,2},{7,3},{8,12},{9,13},{10,... | collective-permute-start | bytes 3145736 | tf_op jit(solution)/shard_map/ppermute | solution.py:55
  135.5 7.1 %collective-permute-start.8 = (bf16[128,4096]{1,0:T(8,128)(2,1)S(1)}, bf16[128,4096]{1,0:T(8,128)(2,1)}, u32[]{:S(2)}, u32[]{:S(2)}) collective-permute-start(bf16[128,4096]{1,0:T(8,128)(2,1)S(1)} %get-tuple-element.28), channel_id=1, source_target_pairs={{0,6},{1,7},{2,0},{3,1},{4,2},{5,3},{6,4},{7,5},{8,14},{9,15},{10,... | collective-permute-start | bytes 3145736 | tf_op jit(solution)/shard_map/ppermute | solution.py:55
  142.5 0.9 collective-permute-start.7
  143.4 15.1 %epilogue.1 = (bf16[2,18,24,1024]{3,2,1,0:T(8,128)(2,1)}, bf16[2,18,24,1024]{3,2,1,0:T(8,128)(2,1)}) custom-call(bf16[864,1024]{1,0:T(8,128)(2,1)} %get-tuple-element.18.att_ref, bf16[3,864,1024]{2,1,0:T(8,128)(2,1)} %get-tuple-element.19.gp_ref, bf16[1024,1024]{1,0:T(8,128)(2,1)} %wo_ref.3, bf16[1024,3072]{1,0:T(8,128)(2,1)} %w_ref.1, ...), custom_call_target="tpu_custom_call" | custom-call | tf_op jit(solution)/shard_map/epilogue/pallas_call | solution.py:251
  158.5 1.4 collective-permute-done.9
  159.9 29.8 %collective-permute-done.8 = bf16[128,4096]{1,0:T(8,128)(2,1)} collective-permute-done((bf16[128,4096]{1,0:T(8,128)(2,1)S(1)}, bf16[128,4096]{1,0:T(8,128)(2,1)}, u32[]{:S(2)}, u32[]{:S(2)}) %collective-permute-start.8) | collective-permute-done | bytes 1048608 | tf_op jit(solution)/shard_map/ppermute | solution.py:55
  189.6 2.7 %fusion.3 = bf16[128,4096]{1,0:T(8,128)(2,1)S(1)} fusion(bf16[128,4096]{1,0:T(8,128)(2,1)S(1)} %collective-permute-done.9, bf16[128,4096]{1,0:T(8,128)(2,1)} %collective-permute-done.8, bf16[128,4096]{1,0:T(8,128)(2,1)} %collective-permute-done.7, bf16[4,128,4096]{2,1,0:T(8,128)(2,1)} %bitcast.65, s32[]{:T(128)S(6)} %select_n.146), kind=kLoop, calls=%fused_computation.11 | loop fusion | flops 4194304 | bytes 5242884 | tf_op jit(solution)/shard_map/convert_element_type | solution.py:316
  192.5 3.4 %collective-permute-start.11 = (bf16[32,4096]{1,0:T(8,128)(2,1)S(1)}, bf16[32,4096]{1,0:T(8,128)(2,1)S(1)}, u32[]{:S(2)}, u32[]{:S(2)}) collective-permute-start(bf16[32,4096]{1,0:T(8,128)(2,1)S(1)} %get-tuple-element.31), channel_id=1, source_target_pairs={{0,48},{1,49},{2,50},{3,51},{4,52},{5,53},{6,54},{7,55},{8,56},{9,... | collective-permute-start | bytes 786440 | tf_op jit(solution)/shard_map/ppermute | solution.py:55
  195.9 0.8 collective-permute-start.10
  196.9 0.8 copy.29
  197.8 2.1 collective-permute-start.4
  200.0 3.2 %collective-permute-done.12 = bf16[32,4096]{1,0:T(8,128)(2,1)S(1)} collective-permute-done((bf16[32,4096]{1,0:T(8,128)(2,1)S(1)}, bf16[32,4096]{1,0:T(8,128)(2,1)S(1)}, u32[]{:S(2)}, u32[]{:S(2)}) %collective-permute-start.12) | collective-permute-done | bytes 262176 | tf_op jit(solution)/shard_map/ppermute | solution.py:55
  203.2 4.6 %collective-permute-done.11 = bf16[32,4096]{1,0:T(8,128)(2,1)S(1)} collective-permute-done((bf16[32,4096]{1,0:T(8,128)(2,1)S(1)}, bf16[32,4096]{1,0:T(8,128)(2,1)S(1)}, u32[]{:S(2)}, u32[]{:S(2)}) %collective-permute-start.11) | collective-permute-done | bytes 262176 | tf_op jit(solution)/shard_map/ppermute | solution.py:55
  208.0 3.1 %collective-permute-start.15 = (bf16[8,4096]{1,0:T(8,128)(2,1)S(1)}, bf16[8,4096]{1,0:T(8,128)(2,1)S(1)}, u32[]{:S(2)}, u32[]{:S(2)}) collective-permute-start(bf16[8,4096]{1,0:T(8,128)(2,1)S(1)} %get-tuple-element.33), channel_id=1, source_target_pairs={{0,8},{1,9},{2,10},{3,11},{4,12},{5,13},{6,14},{7,15},{8,0},{9,1},... | collective-permute-start | bytes 196616 | tf_op jit(solution)/shard_map/ppermute | solution.py:55
  211.1 1.5 collective-permute-start.14
  212.6 4.6 %collective-permute-done.3 = bf16[2,2,15,6,1024]{4,1,3,2,0:T(2,128)(2,1)S(1)} collective-permute-done((bf16[2,2,15,6,1024]{4,1,3,2,0:T(2,128)(2,1)S(1)}, bf16[2,2,15,6,1024]{4,1,3,2,0:T(2,128)(2,1)S(1)}, u32[]{:S(2)}, u32[]{:S(2)}) %collective-permute-start.3) | collective-permute-done | bytes 737312 | tf_op jit(solution)/shard_map/ppermute | solution.py:63
  217.2 1.6 collective-permute-start.13
  218.8 1.2 copy.30.cols_ref
  220.0 0.5 collective-permute-done.5.corner_ref
  220.5 2.9 %collective-permute-done.4.rows_ref = bf16[2,2,3,24,1024]{4,3,2,1,0:T(8,128)(2,1)S(1)} collective-permute-done((bf16[2,2,3,24,1024]{4,3,2,1,0:T(8,128)(2,1)S(1)}, bf16[2,2,3,24,1024]{4,3,2,1,0:T(8,128)(2,1)S(1)}, u32[]{:S(2)}, u32[]{:S(2)}) %collective-permute-start.4) | collective-permute-done | bytes 589856 | tf_op jit(solution)/shard_map/ppermute | solution.py:63
  223.4 0.9 copy-done.5
  224.3 4.7 %restore.1 = (bf16[2,18,24,1024]{3,2,1,0:T(8,128)(2,1)}, bf16[2,18,24,1024]{3,2,1,0:T(8,128)(2,1)}) custom-call(bf16[2,18,24,1024]{3,2,1,0:T(8,128)(2,1)} %get-tuple-element.21.out_ref, bf16[2,18,24,1024]{3,2,1,0:T(8,128)(2,1)} %get-tuple-element.22.grad_ref, bf16[2,2,15,6,1024]{4,3,2,1,0:T(8,128)(2,1)} %copy.30.cols_ref, ...), custom_call_target="tpu_custom_call" | custom-call | tf_op jit(solution)/shard_map/restore/pallas_call | solution.py:285
  229.0 0.6 slice.36
  229.7 0.6 slice.37
  (36 shorter events, 1.0 us)
Async XLA Ops:
  0.6 8.9 %copy-start.1 = (bf16[2,18,24,1024]{3,2,1,0:T(8,128)(2,1)S(1)}, bf16[2,18,24,1024]{3,2,1,0:T(8,128)(2,1)}, u32[]{:S(2)}) copy-start(bf16[2,18,24,1024]{3,2,1,0:T(8,128)(2,1)} %grad_ref.1) | copy-start | bytes 5308420
  2.1 7.4 %copy-start = (bf16[2,18,24,1024]{3,2,1,0:T(8,128)(2,1)S(1)}, bf16[2,18,24,1024]{3,2,1,0:T(8,128)(2,1)}, u32[]{:S(2)}) copy-start(bf16[2,18,24,1024]{3,2,1,0:T(8,128)(2,1)} %lat_ref.1) | copy-start | bytes 5308420
  4.0 17.5 %collective-permute-start = (bf16[2,2,18,6,1024]{4,1,3,2,0:T(2,128)(2,1)}, bf16[2,2,18,6,1024]{4,1,3,2,0:T(2,128)(2,1)}, u32[]{:S(2)}, u32[]{:S(2)}) collective-permute-start(bf16[2,2,18,6,1024]{4,1,3,2,0:T(2,128)(2,1)} %copy.26), channel_id=1, source_target_pairs={{0,15},{1,0},{2,1},{3,2},{4,3},{5,4},{6,5},{7,6},{8,7},{9,8},{10,9... | collective-permute-start | bytes 2654216 | tf_op jit(solution)/shard_map/ppermute | solution.py:63
  10.4 3.8 %copy-start.4 = (bf16[16,20736]{1,0:T(8,128)(2,1)S(1)}, bf16[16,20736]{1,0:T(8,128)(2,1)}, u32[]{:S(2)}) copy-start(bf16[16,20736]{1,0:T(8,128)(2,1)} %param.11) | copy-start | bytes 1990660
  10.4 16.6 %collective-permute-start.1 = (bf16[2,2,3,24,1024]{4,3,2,1,0:T(8,128)(2,1)}, bf16[2,2,3,24,1024]{4,3,2,1,0:T(8,128)(2,1)}, u32[]{:S(2)}, u32[]{:S(2)}) collective-permute-start(bf16[2,2,3,24,1024]{4,3,2,1,0:T(8,128)(2,1)} %fusion.5), channel_id=1, source_target_pairs={{0,112},{1,113},{2,114},{3,115},{4,116},{5,117},{6,118},{7,119},{8... | collective-permute-start | bytes 1769480 | tf_op jit(solution)/shard_map/ppermute | solution.py:63
  13.9 10.1 %collective-permute-start.2 = (bf16[2,2,3,6,1024]{4,3,2,1,0:T(8,128)(2,1)S(1)}, bf16[2,2,3,6,1024]{4,3,2,1,0:T(8,128)(2,1)S(1)}, u32[]{:S(2)}, u32[]{:S(2)}) collective-permute-start(bf16[2,2,3,6,1024]{4,3,2,1,0:T(8,128)(2,1)S(1)} %pad_maximum_fusion.4), channel_id=1, source_target_pairs={{0,127},{1,112},{2,113},{3,114},{4,115},{5,116},{6,117},{7,118},{8... | collective-permute-start | bytes 442376 | tf_op jit(solution)/shard_map/ppermute | solution.py:63
  24.0 3.1 %copy-start.6 = (bf16[2,2,3,6,1024]{4,3,2,1,0:T(8,128)(2,1)}, bf16[2,2,3,6,1024]{4,3,2,1,0:T(8,128)(2,1)S(1)}, u32[]{:S(2)}) copy-start(bf16[2,2,3,6,1024]{4,3,2,1,0:T(8,128)(2,1)S(1)} %collective-permute-done.2.corner_ref) | copy-start | bytes 442372
  108.6 7.5 %collective-permute-start.6 = (bf16[512,4096]{0,1:T(8,128)(2,1)}, bf16[512,4096]{0,1:T(8,128)(2,1)}, u32[]{:S(2)}, u32[]{:S(2)}) collective-permute-start(bf16[512,4096]{0,1:T(8,128)(2,1)} %dynamic-slice_bitcast_fusion), channel_id=1, source_target_pairs={{0,1},{1,0},{2,3},{3,2},{4,5},{5,4},{6,7},{7,6},{8,9},{9,8},{10,11... | collective-permute-start | bytes 12582920 | tf_op jit(solution)/shard_map/ppermute | solution.py:55
  132.1 27.7 %collective-permute-start.9 = (bf16[128,4096]{1,0:T(8,128)(2,1)}, bf16[128,4096]{1,0:T(8,128)(2,1)S(1)}, u32[]{:S(2)}, u32[]{:S(2)}) collective-permute-start(bf16[128,4096]{1,0:T(8,128)(2,1)} %get-tuple-element.27), channel_id=1, source_target_pairs={{0,4},{1,5},{2,6},{3,7},{4,0},{5,1},{6,2},{7,3},{8,12},{9,13},{10,... | collective-permute-start | bytes 3145736 | tf_op jit(solution)/shard_map/ppermute | solution.py:55
  135.5 54.1 %collective-permute-start.8 = (bf16[128,4096]{1,0:T(8,128)(2,1)S(1)}, bf16[128,4096]{1,0:T(8,128)(2,1)}, u32[]{:S(2)}, u32[]{:S(2)}) collective-permute-start(bf16[128,4096]{1,0:T(8,128)(2,1)S(1)} %get-tuple-element.28), channel_id=1, source_target_pairs={{0,6},{1,7},{2,0},{3,1},{4,2},{5,3},{6,4},{7,5},{8,14},{9,15},{10,... | collective-permute-start | bytes 3145736 | tf_op jit(solution)/shard_map/ppermute | solution.py:55
  142.5 47.1 %collective-permute-start.7 = (bf16[128,4096]{1,0:T(8,128)(2,1)S(1)}, bf16[128,4096]{1,0:T(8,128)(2,1)}, u32[]{:S(2)}, u32[]{:S(2)}) collective-permute-start(bf16[128,4096]{1,0:T(8,128)(2,1)S(1)} %get-tuple-element.26), channel_id=1, source_target_pairs={{0,2},{1,3},{2,4},{3,5},{4,6},{5,7},{6,0},{7,1},{8,10},{9,11},{10,... | collective-permute-start | bytes 3145736 | tf_op jit(solution)/shard_map/ppermute | solution.py:55
  189.6 7.0 %copy-start.2 = (bf16[2,18,24,1024]{3,2,1,0:T(8,128)(2,1)S(1)}, bf16[2,18,24,1024]{3,2,1,0:T(8,128)(2,1)}, u32[]{:S(2)}) copy-start(bf16[2,18,24,1024]{3,2,1,0:T(8,128)(2,1)} %get-tuple-element.21.out_ref) | copy-start | bytes 5308420
  189.6 7.0 %copy-start.3 = (bf16[2,18,24,1024]{3,2,1,0:T(8,128)(2,1)S(1)}, bf16[2,18,24,1024]{3,2,1,0:T(8,128)(2,1)}, u32[]{:S(2)}) copy-start(bf16[2,18,24,1024]{3,2,1,0:T(8,128)(2,1)} %get-tuple-element.22.grad_ref) | copy-start | bytes 5308420
  192.4 10.8 %collective-permute-start.12 = (bf16[32,4096]{1,0:T(8,128)(2,1)S(1)}, bf16[32,4096]{1,0:T(8,128)(2,1)S(1)}, u32[]{:S(2)}, u32[]{:S(2)}) collective-permute-start(bf16[32,4096]{1,0:T(8,128)(2,1)S(1)} %get-tuple-element.30), channel_id=1, source_target_pairs={{0,32},{1,33},{2,34},{3,35},{4,36},{5,37},{6,38},{7,39},{8,40},{9,... | collective-permute-start | bytes 786440 | tf_op jit(solution)/shard_map/ppermute | solution.py:55
  192.5 15.3 %collective-permute-start.11 = (bf16[32,4096]{1,0:T(8,128)(2,1)S(1)}, bf16[32,4096]{1,0:T(8,128)(2,1)S(1)}, u32[]{:S(2)}, u32[]{:S(2)}) collective-permute-start(bf16[32,4096]{1,0:T(8,128)(2,1)S(1)} %get-tuple-element.31), channel_id=1, source_target_pairs={{0,48},{1,49},{2,50},{3,51},{4,52},{5,53},{6,54},{7,55},{8,56},{9,... | collective-permute-start | bytes 786440 | tf_op jit(solution)/shard_map/ppermute | solution.py:55
  195.9 11.9 %collective-permute-start.10 = (bf16[32,4096]{1,0:T(8,128)(2,1)S(1)}, bf16[32,4096]{1,0:T(8,128)(2,1)S(1)}, u32[]{:S(2)}, u32[]{:S(2)}) collective-permute-start(bf16[32,4096]{1,0:T(8,128)(2,1)S(1)} %get-tuple-element.29), channel_id=1, source_target_pairs={{0,16},{1,17},{2,18},{3,19},{4,20},{5,21},{6,22},{7,23},{8,24},{9,... | collective-permute-start | bytes 786440 | tf_op jit(solution)/shard_map/ppermute | solution.py:55
  197.7 19.5 %collective-permute-start.3 = (bf16[2,2,15,6,1024]{4,1,3,2,0:T(2,128)(2,1)S(1)}, bf16[2,2,15,6,1024]{4,1,3,2,0:T(2,128)(2,1)S(1)}, u32[]{:S(2)}, u32[]{:S(2)}) collective-permute-start(bf16[2,2,15,6,1024]{4,1,3,2,0:T(2,128)(2,1)S(1)} %copy.29), channel_id=1, source_target_pairs={{0,1},{1,2},{2,3},{3,4},{4,5},{5,6},{6,7},{7,8},{8,9},{9,10},{10,1... | collective-permute-start | bytes 2211848 | tf_op jit(solution)/shard_map/ppermute | solution.py:63
  197.8 25.6 %collective-permute-start.4 = (bf16[2,2,3,24,1024]{4,3,2,1,0:T(8,128)(2,1)S(1)}, bf16[2,2,3,24,1024]{4,3,2,1,0:T(8,128)(2,1)S(1)}, u32[]{:S(2)}, u32[]{:S(2)}) collective-permute-start(bf16[2,2,3,24,1024]{4,3,2,1,0:T(8,128)(2,1)S(1)} %pad_maximum_fusion.2), channel_id=1, source_target_pairs={{0,16},{1,17},{2,18},{3,19},{4,20},{5,21},{6,22},{7,23},{8,24},{9,... | collective-permute-start | bytes 1769480 | tf_op jit(solution)/shard_map/ppermute | solution.py:63
  203.2 17.3 %collective-permute-start.5 = (bf16[2,2,3,6,1024]{4,3,2,1,0:T(8,128)(2,1)S(1)}, bf16[2,2,3,6,1024]{4,3,2,1,0:T(8,128)(2,1)S(1)}, u32[]{:S(2)}, u32[]{:S(2)}) collective-permute-start(bf16[2,2,3,6,1024]{4,3,2,1,0:T(8,128)(2,1)S(1)} %pad_maximum_fusion.3), channel_id=1, source_target_pairs={{0,17},{1,18},{2,19},{3,20},{4,21},{5,22},{6,23},{7,24},{8,25},{9,... | collective-permute-start | bytes 442376 | tf_op jit(solution)/shard_map/ppermute | solution.py:63
  208.0 21.0 %collective-permute-start.15 = (bf16[8,4096]{1,0:T(8,128)(2,1)S(1)}, bf16[8,4096]{1,0:T(8,128)(2,1)S(1)}, u32[]{:S(2)}, u32[]{:S(2)}) collective-permute-start(bf16[8,4096]{1,0:T(8,128)(2,1)S(1)} %get-tuple-element.33), channel_id=1, source_target_pairs={{0,8},{1,9},{2,10},{3,11},{4,12},{5,13},{6,14},{7,15},{8,0},{9,1},... | collective-permute-start | bytes 196616 | tf_op jit(solution)/shard_map/ppermute | solution.py:55
  211.1 17.9 %collective-permute-start.14 = (bf16[8,4096]{1,0:T(8,128)(2,1)S(1)}, bf16[8,4096]{1,0:T(8,128)(2,1)S(1)}, u32[]{:S(2)}, u32[]{:S(2)}) collective-permute-start(bf16[8,4096]{1,0:T(8,128)(2,1)S(1)} %get-tuple-element.34), channel_id=1, source_target_pairs={{0,72},{1,73},{2,74},{3,75},{4,76},{5,77},{6,78},{7,79},{8,64},{9,... | collective-permute-start | bytes 196616 | tf_op jit(solution)/shard_map/ppermute | solution.py:55
  217.2 11.8 %collective-permute-start.13 = (bf16[8,4096]{1,0:T(8,128)(2,1)S(1)}, bf16[8,4096]{1,0:T(8,128)(2,1)S(1)}, u32[]{:S(2)}, u32[]{:S(2)}) collective-permute-start(bf16[8,4096]{1,0:T(8,128)(2,1)S(1)} %get-tuple-element.32), channel_id=1, source_target_pairs={{0,64},{1,65},{2,66},{3,67},{4,68},{5,69},{6,70},{7,71},{8,72},{9,... | collective-permute-start | bytes 196616 | tf_op jit(solution)/shard_map/ppermute | solution.py:55
  220.5 2.9 %copy-start.7 = (bf16[2,2,3,6,1024]{4,3,2,1,0:T(8,128)(2,1)}, bf16[2,2,3,6,1024]{4,3,2,1,0:T(8,128)(2,1)S(1)}, u32[]{:S(2)}) copy-start(bf16[2,2,3,6,1024]{4,3,2,1,0:T(8,128)(2,1)S(1)} %collective-permute-done.5.corner_ref) | copy-start | bytes 442372
  223.4 0.9 copy-start.5

commit v2 on v1

v2 whole, which is shorter than its diff:
```python
import jax
import jax.numpy as jnp
from jax import lax
from jax.experimental import pallas as pl
from jax.experimental.pallas import tpu as pltpu
from jax.sharding import PartitionSpec as P

f32 = jnp.float32
bf16 = jnp.bfloat16
D = 1024
HEADS = 16
QUADS = 4
QW = 256
WIN = 144
TOK = 864
LANES = 4 * WIN
BLOCKED = -1e9
EPS = 1e-05


def nt(a, b):
    return lax.dot_general(a, b, (((1,), (1,)), ((), ())), preferred_element_type=f32)


def tn(a, b):
    return lax.dot_general(a, b, (((0,), (0,)), ((), ())), preferred_element_type=f32)


def nn(a, b):
    return jnp.dot(a, b, preferred_element_type=f32)


def index_of(x, y, z, c):
    return ((z % 2) * 4 + y) * 16 + (z // 2) * 8 + x * 2 + c


def place_of(index):
    lat, lon = index // 16, index % 16
    return dict(x=(lon // 2) % 4, y=lat % 4, z=(lon // 8) * 2 + lat // 4, c=lon % 2)


def my_place(axis):
    lat, lon = lax.axis_index("lat"), lax.axis_index("lon")
    return dict(x=(lon // 2) % 4, y=lat % 4, z=(lon // 8) * 2 + lat // 4, c=lon % 2)[axis]


def shift(value, axis, by):
    size = 2 if axis == "c" else 4
    pairs = []
    for src in range(128):
        place = place_of(src)
        place[axis] = (place[axis] + by) % size
        pairs.append((src, index_of(**place)))
    return lax.ppermute(value, ("lat", "lon"), pairs)


def shift_grid(value, dlat, dlon):
    pairs = []
    for lat in range(8):
        for lon in range(16):
            pairs.append((lat * 16 + lon, ((lat + dlat) % 8) * 16 + (lon + dlon) % 16))
    return lax.ppermute(value, ("lat", "lon"), pairs)


RINGS = ("xyz", "yxz")


def relative_rows():
    owner = place_of(jnp.arange(128, dtype=jnp.int32))
    off = {axis: (owner[axis] - my_place(axis)) % 4 for axis in "xyz"}
    along = [(off[a] * 4 + off[b]) * 4 + off[c] for a, b, c in RINGS]
    return (owner["c"] - my_place("c")) % 2 * 64 + jnp.where(owner["c"] == 0, along[0], along[1])


def ring_shift(value, stage, by):
    pairs = []
    for src in range(128):
        place = place_of(src)
        axis = RINGS[place["c"]][stage]
        place[axis] = (place[axis] + by) % 4
        pairs.append((src, index_of(**place)))
    return lax.ppermute(value, ("lat", "lon"), pairs)


def ring(pieces, stage):
    return [ring_shift(pieces[1], stage, 1), ring_shift(pieces[3], stage, -1), ring_shift(pieces[2], stage, 2)]


def params(mib):
    return pltpu.CompilerParams(vmem_limit_bytes=mib * 1024 * 1024)


def once(shape):
    return pl.BlockSpec(shape, lambda *_: (0,) * len(shape), pipeline_mode=pl.Buffered(1))


def cost(us):
    return pl.CostEstimate(flops=int(us * 1e9), bytes_accessed=int(us * 3e5), transcendentals=0)


def shaped(shape, dtype=bf16):
    return jax.ShapeDtypeStruct(shape, dtype)


VMEM = pl.BlockSpec(memory_space=pltpu.VMEM)
SMEM = pl.BlockSpec(memory_space=pltpu.SMEM)
COLS, ROWS, CORNER = 432, 288, 80


def strips_kernel(lat_ref, grad_ref, cols_ref, rows_ref, corner_ref, cs, rs, ks):
    ks[72:80] = jnp.zeros((8, D), f32)
    for which, tile in enumerate((lat_ref, grad_ref)):
        for l in range(2):
            for i in range(18):
                line = tile[l, i].astype(f32)
                at = (which * 2 + l) * 18 + i
                cs[at * 6 : at * 6 + 6] = line[:6]
                if i < 3:
                    at = (which * 2 + l) * 3 + i
                    rs[at * 24 : at * 24 + 24] = line
                    ks[at * 6 : at * 6 + 6] = line[:6]
    cols_ref[...] = cs[...].astype(bf16)
    rows_ref[...] = rs[...].astype(bf16)
    corner_ref[...] = ks[...].astype(bf16)


def strips(latent, grad_latent):
    return pl.pallas_call(
        strips_kernel,
        in_specs=[VMEM] * 2,
        out_specs=[VMEM] * 3,
        out_shape=[shaped((COLS, D)), shaped((ROWS, D)), shaped((CORNER, D))],
        scratch_shapes=[pltpu.VMEM((n, D), f32) for n in (COLS, ROWS, CORNER)],
        compiler_params=params(20),
        cost_estimate=cost(3),
        name="strips",
    )(latent, grad_latent)


def turned(value, place_ref, first, store):
    t = value.T
    for p in range(t.shape[0] // 8):
        store[pl.ds(pl.multiple_of(place_ref[first + p] * 8, 8), 8)] = t[8 * p : 8 * p + 8]


def prologue_kernel(
    place_ref, lat_ref, grad_ref, cols_ref, rows_ref, corner_ref, gain_ref, xw_ref, gw_ref, nt_ref, n_ref, xs, gs, ts, cs, ks
):
    cs[...] = cols_ref[...].astype(f32)
    ks[...] = corner_ref[...].astype(f32)
    for which, (tile, store) in enumerate(((lat_ref, xs), (grad_ref, gs))):
        for l in range(2):
            for i in range(18):
                if i < 15:
                    main = tile[l, i + 3].astype(f32)
                    at = ((which * 2 + l) * 18 + i + 3) * 6
                    side = cs[at : at + 6]
                else:
                    at = (which * 2 + l) * 3 + i - 15
                    main = rows_ref[at * 24 : at * 24 + 24].astype(f32)
                    side = ks[at * 6 : at * 6 + 6]
                left = (i // 6) * 2 * WIN + l * 72 + (i % 6) * 12
                right = left + WIN
                store[left : left + 12] = main[6:18]
                store[right : right + 6] = main[18:24]
                store[right + 6 : right + 12] = side
    gain = gain_ref[...]
    for w in range(6):
        rows = pl.ds(w * WIN, WIN)
        x = xs[rows]
        centred = x - jnp.mean(x, -1, keepdims=True)
        inv_std = lax.rsqrt(jnp.mean(centred * centred, -1, keepdims=True) + EPS)
        xw_ref[rows] = x.astype(bf16)
        gw_ref[rows] = gs[rows].astype(bf16)
        normed = centred * inv_std * gain
        n_ref[rows] = normed.astype(bf16)
        xs[rows] = normed
    for g in range(4):
        turned(xs[:, g * QW : (g + 1) * QW], place_ref, g * 32, ts)
    nt_ref[...] = ts[...].astype(bf16)


def prologue(place, latent, grad_latent, cols, rows, corner, gain):
    return pl.pallas_call(
        prologue_kernel,
        in_specs=[SMEM] + [VMEM] * 6,
        out_specs=[VMEM] * 4,
        out_shape=[shaped((TOK, D)), shaped((TOK, D)), shaped((D, TOK)), shaped((TOK, D))],
        scratch_shapes=[
            pltpu.VMEM((TOK, D), f32), pltpu.VMEM((TOK, D), f32), pltpu.VMEM((D, TOK), f32),
            pltpu.VMEM((COLS, D), f32), pltpu.VMEM((CORNER, D), f32),
        ],
        compiler_params=params(34),
        cost_estimate=cost(7),
        name="prologue",
    )(place, latent, grad_latent, cols, rows, corner, gain)


def attention(pole, n_ref, gw_ref, wq_ref, wk_ref, wv_ref, wo_ref, bias_ref, att_ref, gp_ref, q, k, v, da):
    n = n_ref[...]
    q[...] = nn(n, wq_ref[...]).astype(bf16)
    k[...] = nn(n, wk_ref[...]).astype(bf16)
    v[...] = nn(n, wv_ref[...]).astype(bf16)
    da[...] = nt(gw_ref[...], wo_ref[...]).astype(bf16)
    lane_head = lax.broadcasted_iota(jnp.int32, (WIN, QW), 1) // 64

    def apart(value):
        zero = jnp.zeros_like(value)
        return jnp.concatenate([jnp.where(lane_head == h, value, zero) for h in range(4)], 0)

    def gathered(stacked):
        out = stacked[:WIN]
        for h in range(1, 4):
            out = jnp.where(lane_head == h, stacked[h * WIN : (h + 1) * WIN], out)
        return out

    def window(w, carry):
        rows = pl.ds(pl.multiple_of(w * WIN, WIN), WIN)
        variant = jnp.where(w >= 4, pole, 0)
        qw, kw, vw, dw = q[rows], k[rows], v[rows], da[rows]
        q_apart = apart(qw * jnp.asarray(0.125, bf16))
        d_apart = apart(dw)
        s = nt(kw, q_apart) + bias_ref[variant, 0].astype(f32)
        e = jnp.exp(s - jnp.max(s, 0, keepdims=True))
        soft = e * (1.0 / jnp.sum(e, 0, keepdims=True))
        soft_b = soft.astype(bf16)
        att_ref[rows] = gathered(tn(soft_b, vw)).astype(bf16)
        dv = nn(soft_b, d_apart)
        dp = nt(vw, d_apart)
        inner = jnp.sum(soft * dp, 0, keepdims=True)
        ds = (soft * (dp - inner)).astype(bf16)
        dk = nn(ds, q_apart)
        dq = gathered(tn(ds, kw)) * 0.125
        gp_ref[0, rows] = dq.astype(bf16)
        gp_ref[1, rows] = dk.astype(bf16)
        gp_ref[2, rows] = dv.astype(bf16)
        return carry

    lax.fori_loop(0, 6, window, 0)


def split_rows(value, keep_ref, send_ref, at):
    keep_ref[:, at : at + QW] = value[:512].astype(bf16)
    send_ref[:, at : at + QW] = value[512:].astype(bf16)


def quads_kernel(
    pole_ref, n_ref, nt_ref, gw_ref, wq_ref, wk_ref, wv_ref, wo_ref, bias_ref,
    att_ref, gp_ref, keep_ref, send_ref, q, k, v, da,
):
    attention(pole_ref[0], n_ref, gw_ref, wq_ref, wk_ref, wv_ref, wo_ref, bias_ref, att_ref, gp_ref, q, k, v, da)
    for part in range(3):
        split_rows(nn(nt_ref[...], gp_ref[part]), keep_ref, send_ref, part * QW)


def out_grads_kernel(place_ref, before_ref, after_ref, gw_ref, keep_ref, send_ref, ts):
    for g in range(4):
        att = before_ref[:, g * QW : (g + 1) * QW] if g < 3 else after_ref[...]
        turned(att.astype(f32), place_ref, g * 32, ts)
    turned_att = ts[...].astype(bf16)
    for part in range(4):
        at = part * QW
        split_rows(nn(turned_att, gw_ref[:, at : at + QW]), keep_ref, send_ref, at)


FIRST = 3


def quad_specs(first):
    def columns(part):
        return pl.BlockSpec((D, QW), lambda g, *_: (0, part * QUADS + first + g))

    return [
        once((TOK, D)), once((D, TOK)), once((TOK, D)),
        columns(0), columns(1), columns(2),
        pl.BlockSpec((QW, D), lambda g, *_: (first + g, 0)),
        pl.BlockSpec((2, 1, WIN, LANES), lambda g, *_: (0, first + g, 0, 0)),
    ]


def some_quads(first, count, pole, normed, normed_t, gw, qkv_weight, out_weight, bias):
    return pl.pallas_call(
        quads_kernel,
        grid_spec=pltpu.PrefetchScalarGridSpec(
            num_scalar_prefetch=1,
            grid=(count,),
            in_specs=quad_specs(first),
            out_specs=[
                pl.BlockSpec((TOK, QW), lambda g, pole: (0, g)),
                pl.BlockSpec((3, TOK, QW), lambda g, pole: (0, 0, g)),
                pl.BlockSpec((512, 3 * QW), lambda g, pole: (0, g)),
                pl.BlockSpec((512, 3 * QW), lambda g, pole: (0, g)),
            ],
            scratch_shapes=[pltpu.VMEM((TOK, QW), bf16)] * 4,
        ),
        out_shape=[
            shaped((TOK, count * QW)), shaped((3, TOK, count * QW)),
            shaped((512, count * 3 * QW)), shaped((512, count * 3 * QW)),
        ],
        compiler_params=params(40),
        cost_estimate=cost(11 * count),
        name="quads",
    )(pole, normed, normed_t, gw, qkv_weight, qkv_weight, qkv_weight, out_weight, bias)


def out_grads(place, before, after, gw):
    return pl.pallas_call(
        out_grads_kernel,
        in_specs=[SMEM] + [VMEM] * 3,
        out_specs=[VMEM] * 2,
        out_shape=[shaped((512, D))] * 2,
        scratch_shapes=[pltpu.VMEM((D, TOK), f32)],
        compiler_params=params(20),
        cost_estimate=cost(7),
        name="out_grads",
    )(place, before, after, gw)


def epilogue_kernel(
    att_ref, att2_ref, gp_ref, gp2_ref, wo_ref, w_ref, xw_ref, gw_ref, gain_ref,
    out_ref, grad_ref, cols_ref, rows_ref, corner_ref, so, sg, cs, rs, ks,
):
    at_first = FIRST * QW
    x = xw_ref[...].astype(f32)
    so[...] = x + nn(att_ref[...], wo_ref[:at_first]) + nn(att2_ref[...], wo_ref[at_first:])
    gn = jnp.zeros((2 * WIN, D), f32)
    for part in range(3):
        gn = gn + nt(gp_ref[part], w_ref[:, part * D : part * D + at_first])
        gn = gn + nt(gp2_ref[part], w_ref[:, part * D + at_first : (part + 1) * D])
    centred = x - jnp.mean(x, -1, keepdims=True)
    inv_std = lax.rsqrt(jnp.mean(centred * centred, -1, keepdims=True) + EPS)
    unit = centred * inv_std
    e = gn * gain_ref[...]
    branch = inv_std * (e - jnp.mean(e, -1, keepdims=True) - unit * jnp.mean(e * unit, -1, keepdims=True))
    sg[...] = gw_ref[...].astype(f32) + branch
    step = pl.program_id(0)
    for which, (src, dst) in enumerate(((so, out_ref), (sg, grad_ref))):
        for l in range(2):
            for r in range(6):
                at = l * 72 + r * 12
                line = jnp.concatenate([src[at : at + 12], src[WIN + at : WIN + at + 12]], 0)
                dst[l, r] = line.astype(bf16)
                to = ((which * 2 + l) * 6 + r) * 6
                cs[to : to + 6] = line[18:]
                if r >= 3:
                    to = (which * 2 + l) * 3 + r - 3
                    rs[to * 24 : to * 24 + 24] = line
                    ks[to * 6 : to * 6 + 6] = line[18:]
    cols_ref[0] = cs[...].astype(bf16)

    @pl.when(step == 2)
    def _():
        ks[72:80] = jnp.zeros((8, D), f32)
        rows_ref[...] = rs[...].astype(bf16)
        corner_ref[...] = ks[...].astype(bf16)


def epilogue(att, att2, gp, gp2, out_weight, qkv_weight, xw, gw, gain):
    rows = 2 * WIN
    tile = pl.BlockSpec((2, 6, 24, D), lambda i: (0, i, 0, 0))
    return pl.pallas_call(
        epilogue_kernel,
        grid=(3,),
        in_specs=[
            pl.BlockSpec((rows, FIRST * QW), lambda i: (i, 0)),
            pl.BlockSpec((rows, QW), lambda i: (i, 0)),
            pl.BlockSpec((3, rows, FIRST * QW), lambda i: (0, i, 0)),
            pl.BlockSpec((3, rows, QW), lambda i: (0, i, 0)),
            once((D, D)),
            once((D, 3 * D)),
            pl.BlockSpec((rows, D), lambda i: (i, 0)),
            pl.BlockSpec((rows, D), lambda i: (i, 0)),
            pl.BlockSpec((1, D), lambda i: (0, 0)),
        ],
        out_specs=[
            tile, tile,
            pl.BlockSpec((1, WIN, D), lambda i: (i, 0, 0)),
            pl.BlockSpec((ROWS, D), lambda i: (0, 0)),
            pl.BlockSpec((CORNER, D), lambda i: (0, 0)),
        ],
        out_shape=[shaped((2, 18, 24, D))] * 2 + [shaped((3, WIN, D)), shaped((ROWS, D)), shaped((CORNER, D))],
        scratch_shapes=[pltpu.VMEM((n, D), f32) for n in (rows, rows, WIN, ROWS, CORNER)],
        compiler_params=params(40),
        cost_estimate=cost(16),
        name="epilogue",
    )(att, att2, gp, gp2, out_weight, qkv_weight, xw, gw, gain)


def restore_kernel(out_ref, grad_ref, cols_ref, rows_ref, corner_ref, updated_ref, back_ref, cs, ks):
    cs[...] = cols_ref[...].astype(f32)
    ks[...] = corner_ref[...].astype(f32)
    for which, (src, dst) in enumerate(((out_ref, updated_ref), (grad_ref, back_ref))):
        for l in range(2):
            for i in range(18):
                if i < 3:
                    at = (which * 2 + l) * 3 + i
                    main = rows_ref[at * 24 : at * 24 + 24].astype(f32)
                    side = ks[at * 6 : at * 6 + 6]
                else:
                    main = src[l, i - 3].astype(f32)
                    at = ((which * 2 + l) * 6 + (i - 3) % 6) * 6
                    side = cs[(i - 3) // 6, at : at + 6]
                dst[l, i] = jnp.concatenate([side, main[:18]], 0).astype(bf16)


def restored(out, grad, cols, rows, corner):
    return pl.pallas_call(
        restore_kernel,
        in_specs=[VMEM] * 5,
        out_specs=[VMEM] * 2,
        out_shape=[shaped((2, 18, 24, D))] * 2,
        scratch_shapes=[pltpu.VMEM((3, WIN, D), f32), pltpu.VMEM((CORNER, D), f32)],
        compiler_params=params(24),
        cost_estimate=cost(5),
        name="restore",
    )(out, grad, cols, rows, corner)


def core_sum_kernel(*refs):
    ins, outs = refs[:-4], refs[-4:]
    at = 0
    for keep, got in zip(ins[::2], ins[1::2]):
        columns = slice(at, at + keep.shape[1])
        for i, out in enumerate(outs):
            rows = slice(i * 128, i * 128 + 128)
            out[:, columns] = (keep[rows].astype(f32) + got[rows].astype(f32)).astype(bf16)
        at += keep.shape[1]


def core_sum(*pairs):
    columns = sum(v.shape[1] for v in pairs[::2])
    return pl.pallas_call(
        core_sum_kernel,
        in_specs=[VMEM] * len(pairs),
        out_specs=[VMEM] * 4,
        out_shape=[shaped((128, columns))] * 4,
        compiler_params=params(16),
        cost_estimate=cost(2),
        name="core_sum",
    )(*pairs)


def summed(refs):
    total = refs[0][...].astype(f32)
    for ref in refs[1:]:
        total = total + ref[...].astype(f32)
    return total


def ring_sum_kernel(*refs):
    ins, outs = refs[:-4], refs[-4:]
    at = 0
    for first in range(0, len(ins), 4):
        total = summed(ins[first : first + 4])
        rows = total.shape[0] // 4
        for i, out in enumerate(outs):
            out[:, at : at + total.shape[1]] = total[i * rows : (i + 1) * rows].astype(out.dtype)
        at += total.shape[1]


def ring_sum(dtype, *groups):
    rows = groups[0][0].shape[0] // 4
    columns = sum(group[0].shape[1] for group in groups)
    return pl.pallas_call(
        ring_sum_kernel,
        in_specs=[VMEM] * (4 * len(groups)),
        out_specs=[VMEM] * 4,
        out_shape=[shaped((rows, columns), dtype)] * 4,
        compiler_params=params(12),
        cost_estimate=cost(1),
        name="ring_sum",
    )(*[v for group in groups for v in group])


def finish_kernel(a, b, c, d, qkv_ref, out_ref):
    total = summed((a, b, c, d)) * (110592.0 ** (-0.5))
    for g in range(4):
        for part in range(3):
            at = (g * 3 + part) * QW
            to = part * D + g * QW
            qkv_ref[:, to : to + QW] = total[:, at : at + QW]
    out_ref[...] = total[:, 3 * D :]


def finish(own, got):
    return pl.pallas_call(
        finish_kernel,
        in_specs=[VMEM] * 4,
        out_specs=[VMEM] * 2,
        out_shape=[shaped((8, 3 * D), f32), shaped((8, D), f32)],
        compiler_params=params(4),
        cost_estimate=cost(1),
        name="finish",
    )(own, *got)


def per_device(latent, grad_latent, qkv_weight, out_weight, norm_gain, pair_bias):
    cols, rows, corner = strips(latent, grad_latent)
    cols = shift_grid(cols, 0, -1)
    rows = shift_grid(rows, -1, 0)
    corner = shift_grid(corner, -1, -1)
    gain = norm_gain.reshape(1, D)

    table = pair_bias.reshape(QUADS, 4, WIN, WIN).transpose(0, 3, 1, 2)
    upper = jnp.arange(WIN) % 72 // 12 >= 3
    differ = upper[:, None, None] != upper[None, None, :]
    bias = jnp.stack([table, jnp.where(differ, jnp.asarray(BLOCKED, bf16), table)])
    bias = bias.reshape(2, QUADS, WIN, LANES)
    pole = (lax.axis_index("lat") == lax.axis_size("lat") - 1).astype(jnp.int32).reshape(1)
    place = relative_rows()

    xw, gw, normed_t, normed = prologue(place, latent, grad_latent, cols, rows, corner, gain)
    att, gp, keep, send = some_quads(0, FIRST, pole, normed, normed_t, gw, qkv_weight, out_weight, bias)
    got = shift(send, "c", 1)
    att2, gp2, keep2, send2 = some_quads(FIRST, 1, pole, normed, normed_t, gw, qkv_weight, out_weight, bias)
    got2 = shift(send2, "c", 1)
    pieces = core_sum(keep, got)
    moved = ring(pieces, 0)
    att2, _ = lax.optimization_barrier((att2, pieces[1]))
    keep3, send3 = out_grads(place, att, att2, gw)
    got3 = shift(send3, "c", 1)
    pieces2 = core_sum(keep2, got2, keep3, got3)
    moved2 = ring(pieces2, 0)
    att2, _ = lax.optimization_barrier((att2, pieces2[1]))
    out_tile, grad_tile, cols, rows, corner = epilogue(
        att, att2, gp, gp2, out_weight, qkv_weight, xw, gw, gain
    )
    cols = shift_grid(cols, 0, 1)
    rows = shift_grid(rows, 1, 0)
    corner = shift_grid(corner, 1, 1)
    pieces = ring_sum(bf16, [pieces[0]] + moved, [pieces2[0]] + moved2)
    pieces = ring_sum(f32, [pieces[0]] + ring(pieces, 1))
    updated, grad_input = restored(out_tile, grad_tile, cols, rows, corner)
    qkv_grad, out_grad = finish(pieces[0], ring(pieces, 2))
    return (updated, grad_input, qkv_grad, out_grad)


def solution(mesh):
    in_specs = (P(None, "lat", "lon", None), P(None, "lat", "lon", None), P(), P(), P(), P())
    out_specs = (
        P(None, "lat", "lon", None),
        P(None, "lat", "lon", None),
        P(("lat", "lon"), None),
        P(("lat", "lon"), None),
    )
    return jax.shard_map(
        per_device, mesh=mesh, in_specs=in_specs, out_specs=out_specs, check_vma=False
    )
```

time: 235 us -> 163 us (0.69); the launches traced: 230 us -> 163 us
  local copies, waits for them, and re-layouts: 38.8 us -> 13.8 us
  waiting for transfers between devices: 57.5 us -> 33.9 us
  other arithmetic: 21.7 us -> 3.29 us
  Pallas kernels: 78 us -> 73.1 us
  starting transfers between devices: 33.4 us -> 38 us
    ppermute x10 -> x3, waiting for transfers between devices: 46.5 us -> 0.01 us  [shift(): return lax.ppermute(value, ('lat', 'lon'), pairs)]
    ppermute x0 -> x12, waiting for transfers between devices: none -> 29.9 us  [ring_shift(): return lax.ppermute(value, ('lat', 'lon'), pairs)]
    ppermute x0 -> x12, starting transfers between devices: none -> 25.7 us  [ring_shift(): return lax.ppermute(value, ('lat', 'lon'), pairs)]
    ppermute x10 -> x3, starting transfers between devices: 21.8 us -> 1.24 us  [shift(): return lax.ppermute(value, ('lat', 'lon'), pairs)]
    transpose x1 -> x0, local copies, waits for them, and re-layouts: 11.5 us -> none  [per_device(): part = part.transpose(0, 2, 1, 3).reshape(2, 512, 4 * D)]
    convert_element_type x2 -> x0, other arithmetic: 9.27 us -> none  [the longest x1 6.61 us: core_stage(): return (pick(v, m).astype(f32) + r.astype(f32)).astype(bf16)]
    squeeze x4 -> x0, local copies, waits for them, and re-layouts: 7.57 us -> none  [pick(): return lax.dynamic_index_in_dim(v, i, 0, keepdims=False)]
    transpose x1 -> x0, other arithmetic: 7.36 us -> none  [per_device(): part = part.transpose(0, 2, 1, 3).reshape(2, 512, 4 * D)]
  transfers between devices with their start and end apart: 16 -> 21, of which waited for: 9 -> 8; matrix products, arithmetic and copies ran while one was open for 6% -> 7% of each run, Pallas kernels for 9% -> 16%
where the time goes in v2:
time: 163 us
  Pallas kernels  73.1 us (45%)
  starting transfers between devices  38 us (23%)
  waiting for transfers between devices  33.9 us (21%)
  local copies, waits for them, and re-layouts  13.8 us (8%)
  other arithmetic  3.29 us (2%)
    pallas_call x2, Pallas kernels, some_quads(): pl.pallas_call(quads_kernel, grid_spec=pltpu.PrefetchScalarGridSpec(num_s...  45.2 us
    ppermute x12, waiting for transfers between devices, ring_shift(): return lax.ppermute(value, ('lat', 'lon'), pairs)  29.9 us
    ppermute x12, starting transfers between devices, ring_shift(): return lax.ppermute(value, ('lat', 'lon'), pairs)  25.7 us
    pallas_call x1, Pallas kernels, epilogue(): pl.pallas_call(epilogue_kernel, grid=(3,), in_specs=[pl.BlockSpec((rows,...  13.5 us
    ppermute x6, starting transfers between devices, shift_grid(): return lax.ppermute(value, ('lat', 'lon'), pairs)  11.1 us
    another operation x3, local copies, waits for them, and re-layouts, per_device(): jnp.stack([table, jnp.where(differ, jnp.asarray(BLOCKED, bf16), table)])  5.32 us
    unnamed x27, local copies, waits for them, and re-layouts  5.03 us
    pallas_call x1, Pallas kernels, prologue(): pl.pallas_call(prologue_kernel, in_specs=[SMEM] + [VMEM] * 6, out_specs=[...  4.98 us
  transfers between devices with their start and end apart: 21, of which 8 were waited for; matrix products, arithmetic and copies ran while one was open for 7% of the time, Pallas kernels for 16%

profile of v2, /device:TPU:0, one launch (start us, length us, event | category | flops | bytes accessed | tf_op | source)
XLA Modules:
  0.0 163.0 jit_solution(16308064425760007439)
XLA Ops:
  0.6 1.5 copy-done.1
  2.1 1.5 copy-done.3
  3.6 1.3 strips.1
  4.9 5.6 %collective-permute-start = (bf16[432,1024]{1,0:T(8,128)(2,1)}, bf16[432,1024]{1,0:T(8,128)(2,1)}, u32[]{:S(2)}, u32[]{:S(2)}) collective-permute-start(bf16[432,1024]{1,0:T(8,128)(2,1)} %get-tuple-element.48), channel_id=1, source_target_pairs={{0,15},{1,0},{2,1},{3,2},{4,3},{5,4},{6,5},{7,6},{8,7},{9,8},{10,9... | collective-permute-start | bytes 2654216 | tf_op jit(solution)/shard_map/ppermute | solution.py:62
  10.5 3.5 %collective-permute-start.1 = (bf16[288,1024]{1,0:T(8,128)(2,1)}, bf16[288,1024]{1,0:T(8,128)(2,1)}, u32[]{:S(2)}, u32[]{:S(2)}) collective-permute-start(bf16[288,1024]{1,0:T(8,128)(2,1)} %get-tuple-element.49), channel_id=1, source_target_pairs={{0,112},{1,113},{2,114},{3,115},{4,116},{5,117},{6,118},{7,119},{8... | collective-permute-start | bytes 1769480 | tf_op jit(solution)/shard_map/ppermute | solution.py:62
  13.9 0.3 collective-permute-start.2
  14.3 2.1 %reshape.81 = bf16[4,4,144,144]{3,2,1,0:T(8,128)(2,1)S(1)} reshape(bf16[16,20736]{1,0:T(8,128)(2,1)S(1)} %copy-done.12) | data formatting | bytes 1327104 | tf_op jit(solution)/shard_map/reshape | solution.py:504
  16.4 1.3 copy.10
  17.7 0.8 stack.9
  18.5 0.7 broadcast_compare_fusion
  19.3 2.5 %broadcast_select_fusion = bf16[4,144,4,144]{3,2,1,0:T(4,128)(2,1)} fusion(pred[144,144]{1,0:T(8,128)(4,1)} %broadcast_compare_fusion, bf16[4,4,144,144]{2,1,3,0:T(4,128)(2,1)S(1)} %copy.10), kind=kLoop, calls=%fused_computation | loop fusion | flops 331776 | bytes 1347840 | tf_op jit(solution)/shard_map/jit(_where)/select_n | solution.py:507
  21.9 3.3 %stack.10 = bf16[1,4,144,576]{3,2,1,0:T(8,128)(2,1)} reshape(bf16[4,144,4,144]{3,2,1,0:T(4,128)(2,1)} %broadcast_select_fusion) | data formatting | bytes 1327104 | tf_op jit(solution)/shard_map/stack | solution.py:507
  25.2 1.2 constant_dynamic-update-slice_fusion.bias_ref
  26.5 1.5 copy-done.4
  28.0 5.0 %prologue.1 = (bf16[864,1024]{1,0:T(8,128)(2,1)S(1)}, bf16[864,1024]{1,0:T(8,128)(2,1)S(1)}, bf16[1024,864]{1,0:T(8,128)(2,1)S(1)}, bf16[864,1024]{1,0:T(8,128)(2,1)S(1)}) custom-call(s32[128]{0:T(128)S(1)} %fusion.2.place_ref, bf16[2,18,24,1024]{3,2,1,0:T(8,128)(2,1)S(1)} %copy-done.2, bf16[2,18,24,1024]{3,2,1,0:T(8,128)(2,1)S(1)} %copy-done.4, ...), custom_call_target="tpu_custom_call" | custom-call | flops 7000000000 | bytes 2100000 | tf_op jit(solution)/shard_map/prologue/pallas_call | solution.py:184
  33.0 33.8 %quads.2 = (bf16[864,768]{1,0:T(8,128)(2,1)S(1)}, bf16[3,864,768]{2,1,0:T(8,128)(2,1)}, bf16[512,2304]{1,0:T(8,128)(2,1)S(1)}, bf16[512,2304]{1,0:T(8,128)(2,1)}) custom-call(s32[1]{0:T(128)} %bitcast.pole_ref, bf16[864,1024]{1,0:T(8,128)(2,1)S(1)} %get-tuple-element.51.n_ref, bf16[1024,864]{1,0:T(8,128)(2,1)S(1)} %get-tuple-element.52.nt_ref, ...), custom_call_target="tpu_custom_call" | custom-call | flops 32999999488 | bytes 9900000 | tf_op jit(solution)/shard_map/quads/pallas_call | solution.py:282
  66.8 0.6 collective-permute-start.3
  67.4 11.4 %quads.3 = (bf16[864,256]{1,0:T(8,128)(2,1)S(1)}, bf16[3,864,256]{2,1,0:T(8,128)(2,1)S(1)}, bf16[512,768]{1,0:T(8,128)(2,1)S(1)}, bf16[512,768]{1,0:T(8,128)(2,1)S(1)}) custom-call(s32[1]{0:T(128)} %bitcast.pole_ref, bf16[864,1024]{1,0:T(8,128)(2,1)S(1)} %get-tuple-element.51.n_ref, bf16[1024,864]{1,0:T(8,128)(2,1)S(1)} %get-tuple-element.52.nt_ref, ...), custom_call_target="tpu_custom_call" | custom-call | flops 11000000512 | bytes 3300000 | tf_op jit(solution)/shard_map/quads/pallas_call | solution.py:282
  78.8 0.5 core_sum.2
  79.4 0.5 copy-done.8
  79.9 3.4 %out_grads.1 = (bf16[512,1024]{1,0:T(8,128)(2,1)S(1)}, bf16[512,1024]{1,0:T(8,128)(2,1)S(1)}) custom-call(s32[128]{0:T(128)S(1)} %fusion.2.place_ref, bf16[864,768]{1,0:T(8,128)(2,1)S(1)} %get-tuple-element.54.before_ref.att_ref, bf16[864,256]{1,0:T(8,128)(2,1)S(1)} %get-tuple-element.65.after_ref.att2_ref, bf16[864,1024]{1,0:T(8,128)(2,1)S(1)} %get-tuple-element.53.gw_ref), custom_call_target="tpu_custom_call" | custom-call | flops 7000000000 | bytes 2100000 | tf_op jit(solution)/shard_map/out_grads/pallas_call | solution.py:307
  83.3 0.6 collective-permute-start.5
  83.9 9.9 %collective-permute-start.10 = (bf16[128,2304]{1,0:T(8,128)(2,1)S(1)}, bf16[128,2304]{1,0:T(8,128)(2,1)S(1)}, u32[]{:S(2)}, u32[]{:S(2)}) collective-permute-start(bf16[128,2304]{1,0:T(8,128)(2,1)S(1)} %get-tuple-element.77), channel_id=1, source_target_pairs={{0,6},{1,49},{2,0},{3,51},{4,2},{5,53},{6,4},{7,55},{8,14},{9,57},... | collective-permute-start | bytes 1769480 | tf_op jit(solution)/shard_map/ppermute | solution.py:82
  93.9 1.5 collective-permute-start.11
  95.3 0.4 core_sum.3
  95.8 2.7 %collective-permute-start.12 = (bf16[128,1792]{1,0:T(8,128)(2,1)S(1)}, bf16[128,1792]{1,0:T(8,128)(2,1)S(1)}, u32[]{:S(2)}, u32[]{:S(2)}) collective-permute-start(bf16[128,1792]{1,0:T(8,128)(2,1)S(1)} %get-tuple-element.64), channel_id=1, source_target_pairs={{0,2},{1,17},{2,4},{3,19},{4,6},{5,21},{6,0},{7,23},{8,10},{9,25},... | collective-permute-start | bytes 1376264 | tf_op jit(solution)/shard_map/ppermute | solution.py:82
  98.5 0.6 collective-permute-start.13
  99.1 8.5 %collective-permute-done.10.refs_2_ = bf16[128,2304]{1,0:T(8,128)(2,1)S(1)} collective-permute-done((bf16[128,2304]{1,0:T(8,128)(2,1)S(1)}, bf16[128,2304]{1,0:T(8,128)(2,1)S(1)}, u32[]{:S(2)}, u32[]{:S(2)}) %collective-permute-start.10) | collective-permute-done | bytes 589856 | tf_op jit(solution)/shard_map/ppermute | solution.py:82
  107.6 13.5 %epilogue.1 = (bf16[2,18,24,1024]{3,2,1,0:T(8,128)(2,1)S(1)}, bf16[2,18,24,1024]{3,2,1,0:T(8,128)(2,1)S(1)}, bf16[3,144,1024]{2,1,0:T(8,128)(2,1)S(1)}, bf16[288...) custom-call(bf16[864,768]{1,0:T(8,128)(2,1)S(1)} %copy-done.11, bf16[864,256]{1,0:T(8,128)(2,1)S(1)} %get-tuple-element.65.after_ref.att2_ref, ...), custom_call_target="tpu_custom_call" | custom-call | flops 16000000000 | bytes 4800000 | tf_op jit(solution)/shard_map/epilogue/pallas_call | solution.py:361
  121.1 0.3 collective-permute-start.6
  121.5 0.5 ring_sum.2
  122.0 0.2 collective-permute-start.15
  122.3 3.4 %collective-permute-start.16 = (bf16[32,4096]{1,0:T(8,128)(2,1)S(1)}, bf16[32,4096]{1,0:T(8,128)(2,1)S(1)}, u32[]{:S(2)}, u32[]{:S(2)}) collective-permute-start(bf16[32,4096]{1,0:T(8,128)(2,1)S(1)} %get-tuple-element.84), channel_id=1, source_target_pairs={{0,48},{1,7},{2,50},{3,1},{4,52},{5,3},{6,54},{7,5},{8,56},{9,15},... | collective-permute-start | bytes 786440 | tf_op jit(solution)/shard_map/ppermute | solution.py:82
  125.7 1.4 collective-permute-start.17
  127.1 1.4 collective-permute-start.7
  128.5 1.5 collective-permute-done.15.refs_1_
  130.0 2.5 %collective-permute-done.16.refs_2_ = bf16[32,4096]{1,0:T(8,128)(2,1)S(1)} collective-permute-done((bf16[32,4096]{1,0:T(8,128)(2,1)S(1)}, bf16[32,4096]{1,0:T(8,128)(2,1)S(1)}, u32[]{:S(2)}, u32[]{:S(2)}) %collective-permute-start.16) | collective-permute-done | bytes 262176 | tf_op jit(solution)/shard_map/ppermute | solution.py:82
  132.4 1.9 %collective-permute-done.17.refs_3_ = bf16[32,4096]{1,0:T(8,128)(2,1)S(1)} collective-permute-done((bf16[32,4096]{1,0:T(8,128)(2,1)S(1)}, bf16[32,4096]{1,0:T(8,128)(2,1)S(1)}, u32[]{:S(2)}, u32[]{:S(2)}) %collective-permute-start.17) | collective-permute-done | bytes 262176 | tf_op jit(solution)/shard_map/ppermute | solution.py:82
  134.3 0.1 ring_sum.3
  134.4 2.0 %collective-permute-start.18 = (f32[8,4096]{1,0:T(8,128)S(1)}, f32[8,4096]{1,0:T(8,128)S(1)}, u32[]{:S(2)}, u32[]{:S(2)}) collective-permute-start(f32[8,4096]{1,0:T(8,128)S(1)} %get-tuple-element.87), channel_id=1, source_target_pairs={{0,64},{1,65},{2,66},{3,67},{4,68},{5,69},{6,70},{7,71},{8,72},{9,... | collective-permute-start | bytes 393224 | tf_op jit(solution)/shard_map/ppermute | solution.py:82
  136.4 1.3 collective-permute-start.19
  137.8 2.7 %collective-permute-start.20 = (f32[8,4096]{1,0:T(8,128)S(1)}, f32[8,4096]{1,0:T(8,128)S(1)}, u32[]{:S(2)}, u32[]{:S(2)}) collective-permute-start(f32[8,4096]{1,0:T(8,128)S(1)} %get-tuple-element.89), channel_id=1, source_target_pairs={{0,8},{1,9},{2,10},{3,11},{4,12},{5,13},{6,14},{7,15},{8,0},{9,1},... | collective-permute-start | bytes 393224 | tf_op jit(solution)/shard_map/ppermute | solution.py:82
  140.4 10.0 %collective-permute-done.18.b = f32[8,4096]{1,0:T(8,128)S(1)} collective-permute-done((f32[8,4096]{1,0:T(8,128)S(1)}, f32[8,4096]{1,0:T(8,128)S(1)}, u32[]{:S(2)}, u32[]{:S(2)}) %collective-permute-start.18) | collective-permute-done | bytes 131104 | tf_op jit(solution)/shard_map/ppermute | solution.py:82
  150.4 2.3 %collective-permute-done.19.c = f32[8,4096]{1,0:T(8,128)S(1)} collective-permute-done((f32[8,4096]{1,0:T(8,128)S(1)}, f32[8,4096]{1,0:T(8,128)S(1)}, u32[]{:S(2)}, u32[]{:S(2)}) %collective-permute-start.19) | collective-permute-done | bytes 131104 | tf_op jit(solution)/shard_map/ppermute | solution.py:82
  152.8 3.3 %collective-permute-done.20.d = f32[8,4096]{1,0:T(8,128)S(1)} collective-permute-done((f32[8,4096]{1,0:T(8,128)S(1)}, f32[8,4096]{1,0:T(8,128)S(1)}, u32[]{:S(2)}, u32[]{:S(2)}) %collective-permute-start.20) | collective-permute-done | bytes 131104 | tf_op jit(solution)/shard_map/ppermute | solution.py:82
  156.0 0.7 finish.1
  156.7 3.9 %collective-permute-done.8.corner_ref = bf16[80,1024]{1,0:T(8,128)(2,1)S(1)} collective-permute-done((bf16[80,1024]{1,0:T(8,128)(2,1)S(1)}, bf16[80,1024]{1,0:T(8,128)(2,1)S(1)}, u32[]{:S(2)}, u32[]{:S(2)}) %collective-permute-start.8) | collective-permute-done | bytes 163872 | tf_op jit(solution)/shard_map/ppermute | solution.py:62
  160.6 2.4 %restore.1 = (bf16[2,18,24,1024]{3,2,1,0:T(8,128)(2,1)}, bf16[2,18,24,1024]{3,2,1,0:T(8,128)(2,1)}) custom-call(bf16[2,18,24,1024]{3,2,1,0:T(8,128)(2,1)S(1)} %get-tuple-element.69.out_ref, bf16[2,18,24,1024]{3,2,1,0:T(8,128)(2,1)S(1)} %get-tuple-element.70.grad_ref, bf16[3,144,1024]{2,1,0:T(8,128)(2,1)S(1)} %collective-permute-done.6.cols_ref, ...), custom_call_target="tpu_custom_call" | custom-call | flops 5000000000 | bytes 1500000 | tf_op jit(solution)/shard_map/restore/pallas_call | solution.py:407
  (42 shorter events, 0.3 us)
Async XLA Ops:
  0.6 1.5 copy-start.1
  2.1 1.5 copy-start.3
  3.6 10.7 %copy-start.12 = (bf16[16,20736]{1,0:T(8,128)(2,1)S(1)}, bf16[16,20736]{1,0:T(8,128)(2,1)}, u32[]{:S(2)}) copy-start(bf16[16,20736]{1,0:T(8,128)(2,1)} %param.11) | copy-start | bytes 1990660
  4.9 21.6 %collective-permute-start = (bf16[432,1024]{1,0:T(8,128)(2,1)}, bf16[432,1024]{1,0:T(8,128)(2,1)}, u32[]{:S(2)}, u32[]{:S(2)}) collective-permute-start(bf16[432,1024]{1,0:T(8,128)(2,1)} %get-tuple-element.48), channel_id=1, source_target_pairs={{0,15},{1,0},{2,1},{3,2},{4,3},{5,4},{6,5},{7,6},{8,7},{9,8},{10,9... | collective-permute-start | bytes 2654216 | tf_op jit(solution)/shard_map/ppermute | solution.py:62
  10.5 16.0 %collective-permute-start.1 = (bf16[288,1024]{1,0:T(8,128)(2,1)}, bf16[288,1024]{1,0:T(8,128)(2,1)}, u32[]{:S(2)}, u32[]{:S(2)}) collective-permute-start(bf16[288,1024]{1,0:T(8,128)(2,1)} %get-tuple-element.49), channel_id=1, source_target_pairs={{0,112},{1,113},{2,114},{3,115},{4,116},{5,117},{6,118},{7,119},{8... | collective-permute-start | bytes 1769480 | tf_op jit(solution)/shard_map/ppermute | solution.py:62
  13.9 12.5 %collective-permute-start.2 = (bf16[80,1024]{1,0:T(8,128)(2,1)}, bf16[80,1024]{1,0:T(8,128)(2,1)S(1)}, u32[]{:S(2)}, u32[]{:S(2)}) collective-permute-start(bf16[80,1024]{1,0:T(8,128)(2,1)} %get-tuple-element.50), channel_id=1, source_target_pairs={{0,127},{1,112},{2,113},{3,114},{4,115},{5,116},{6,117},{7,118},{8... | collective-permute-start | bytes 491528 | tf_op jit(solution)/shard_map/ppermute | solution.py:62
  21.9 4.6 %copy-start.2 = (bf16[2,18,24,1024]{3,2,1,0:T(8,128)(2,1)S(1)}, bf16[2,18,24,1024]{3,2,1,0:T(8,128)(2,1)}, u32[]{:S(2)}) copy-start(bf16[2,18,24,1024]{3,2,1,0:T(8,128)(2,1)} %lat_ref.3) | copy-start | bytes 5308420
  21.9 4.6 %copy-start.5 = (f32[1024]{0:T(1024)S(1)}, f32[1024]{0:T(1024)}, u32[]{:S(2)}) copy-start(f32[1024]{0:T(1024)} %param.10) | copy-start | bytes 12292
  26.5 1.5 copy-start.4
  28.0 5.0 %copy-start = (bf16[1024,1024]{1,0:T(8,128)(2,1)S(1)}, bf16[1024,1024]{1,0:T(8,128)(2,1)}, u32[]{:S(2)}) copy-start(bf16[1024,1024]{1,0:T(8,128)(2,1)} %wo_ref.5) | copy-start | bytes 6291460
  33.0 46.9 %copy-start.6 = (bf16[864,1024]{1,0:T(8,128)(2,1)}, bf16[864,1024]{1,0:T(8,128)(2,1)S(1)}, u32[]{:S(2)}) copy-start(bf16[864,1024]{1,0:T(8,128)(2,1)S(1)} %get-tuple-element.53.gw_ref) | copy-start | bytes 5308420
  66.8 13.1 %copy-start.10 = (bf16[864,768]{1,0:T(8,128)(2,1)}, bf16[864,768]{1,0:T(8,128)(2,1)S(1)}, u32[]{:S(2)}) copy-start(bf16[864,768]{1,0:T(8,128)(2,1)S(1)} %get-tuple-element.54.before_ref.att_ref) | copy-start | bytes 3981316
  66.8 12.0 %collective-permute-start.3 = (bf16[512,2304]{1,0:T(8,128)(2,1)}, bf16[512,2304]{1,0:T(8,128)(2,1)S(1)}, u32[]{:S(2)}, u32[]{:S(2)}) collective-permute-start(bf16[512,2304]{1,0:T(8,128)(2,1)} %get-tuple-element.57), channel_id=1, source_target_pairs={{0,1},{1,0},{2,3},{3,2},{4,5},{5,4},{6,7},{7,6},{8,9},{9,8},{10,11... | collective-permute-start | bytes 7077896 | tf_op jit(solution)/shard_map/ppermute | solution.py:54
  78.8 1.1 copy-start.8
  83.3 12.0 %collective-permute-start.5 = (bf16[512,1024]{1,0:T(8,128)(2,1)S(1)}, bf16[512,1024]{1,0:T(8,128)(2,1)S(1)}, u32[]{:S(2)}, u32[]{:S(2)}) collective-permute-start(bf16[512,1024]{1,0:T(8,128)(2,1)S(1)} %get-tuple-element.63), channel_id=1, source_target_pairs={{0,1},{1,0},{2,3},{3,2},{4,5},{5,4},{6,7},{7,6},{8,9},{9,8},{10,11... | collective-permute-start | bytes 3145736 | tf_op jit(solution)/shard_map/ppermute | solution.py:54
  83.8 11.5 %collective-permute-start.4 = (bf16[512,768]{1,0:T(8,128)(2,1)S(1)}, bf16[512,768]{1,0:T(8,128)(2,1)S(1)}, u32[]{:S(2)}, u32[]{:S(2)}) collective-permute-start(bf16[512,768]{1,0:T(8,128)(2,1)S(1)} %get-tuple-element.61), channel_id=1, source_target_pairs={{0,1},{1,0},{2,3},{3,2},{4,5},{5,4},{6,7},{7,6},{8,9},{9,8},{10,11... | collective-permute-start | bytes 2359304 | tf_op jit(solution)/shard_map/ppermute | solution.py:54
  83.9 23.6 %collective-permute-start.10 = (bf16[128,2304]{1,0:T(8,128)(2,1)S(1)}, bf16[128,2304]{1,0:T(8,128)(2,1)S(1)}, u32[]{:S(2)}, u32[]{:S(2)}) collective-permute-start(bf16[128,2304]{1,0:T(8,128)(2,1)S(1)} %get-tuple-element.77), channel_id=1, source_target_pairs={{0,6},{1,49},{2,0},{3,51},{4,2},{5,53},{6,4},{7,55},{8,14},{9,57},... | collective-permute-start | bytes 1769480 | tf_op jit(solution)/shard_map/ppermute | solution.py:82
  93.8 27.6 %collective-permute-start.9 = (bf16[128,2304]{1,0:T(8,128)(2,1)S(1)}, bf16[128,2304]{1,0:T(8,128)(2,1)S(1)}, u32[]{:S(2)}, u32[]{:S(2)}) collective-permute-start(bf16[128,2304]{1,0:T(8,128)(2,1)S(1)} %get-tuple-element.58), channel_id=1, source_target_pairs={{0,2},{1,17},{2,4},{3,19},{4,6},{5,21},{6,0},{7,23},{8,10},{9,25},... | collective-permute-start | bytes 1769480 | tf_op jit(solution)/shard_map/ppermute | solution.py:82
  93.9 27.3 %collective-permute-start.11 = (bf16[128,2304]{1,0:T(8,128)(2,1)S(1)}, bf16[128,2304]{1,0:T(8,128)(2,1)S(1)}, u32[]{:S(2)}, u32[]{:S(2)}) collective-permute-start(bf16[128,2304]{1,0:T(8,128)(2,1)S(1)} %get-tuple-element.78), channel_id=1, source_target_pairs={{0,4},{1,33},{2,6},{3,35},{4,0},{5,37},{6,2},{7,39},{8,12},{9,41},... | collective-permute-start | bytes 1769480 | tf_op jit(solution)/shard_map/ppermute | solution.py:82
  95.3 12.3 %copy-start.7 = (bf16[864,1024]{1,0:T(8,128)(2,1)S(1)}, bf16[864,1024]{1,0:T(8,128)(2,1)}, u32[]{:S(2)}) copy-start(bf16[864,1024]{1,0:T(8,128)(2,1)} %copy-done.6) | copy-start | bytes 5308420
  95.3 12.3 %copy-start.9 = (bf16[3,864,256]{2,1,0:T(8,128)(2,1)S(1)}, bf16[3,864,256]{2,1,0:T(8,128)(2,1)}, u32[]{:S(2)}) copy-start(bf16[3,864,256]{2,1,0:T(8,128)(2,1)} %copy-done.8) | copy-start | bytes 3981316
  95.3 12.2 %copy-start.11 = (bf16[864,768]{1,0:T(8,128)(2,1)S(1)}, bf16[864,768]{1,0:T(8,128)(2,1)}, u32[]{:S(2)}) copy-start(bf16[864,768]{1,0:T(8,128)(2,1)} %copy-done.10) | copy-start | bytes 3981316
  95.8 25.7 %collective-permute-start.12 = (bf16[128,1792]{1,0:T(8,128)(2,1)S(1)}, bf16[128,1792]{1,0:T(8,128)(2,1)S(1)}, u32[]{:S(2)}, u32[]{:S(2)}) collective-permute-start(bf16[128,1792]{1,0:T(8,128)(2,1)S(1)} %get-tuple-element.64), channel_id=1, source_target_pairs={{0,2},{1,17},{2,4},{3,19},{4,6},{5,21},{6,0},{7,23},{8,10},{9,25},... | collective-permute-start | bytes 1376264 | tf_op jit(solution)/shard_map/ppermute | solution.py:82
  98.5 23.0 %collective-permute-start.13 = (bf16[128,1792]{1,0:T(8,128)(2,1)S(1)}, bf16[128,1792]{1,0:T(8,128)(2,1)S(1)}, u32[]{:S(2)}, u32[]{:S(2)}) collective-permute-start(bf16[128,1792]{1,0:T(8,128)(2,1)S(1)} %get-tuple-element.80), channel_id=1, source_target_pairs={{0,6},{1,49},{2,0},{3,51},{4,2},{5,53},{6,4},{7,55},{8,14},{9,57},... | collective-permute-start | bytes 1376264 | tf_op jit(solution)/shard_map/ppermute | solution.py:82
  107.6 13.9 %collective-permute-start.14 = (bf16[128,1792]{1,0:T(8,128)(2,1)S(1)}, bf16[128,1792]{1,0:T(8,128)(2,1)S(1)}, u32[]{:S(2)}, u32[]{:S(2)}) collective-permute-start(bf16[128,1792]{1,0:T(8,128)(2,1)S(1)} %get-tuple-element.81), channel_id=1, source_target_pairs={{0,4},{1,33},{2,6},{3,35},{4,0},{5,37},{6,2},{7,39},{8,12},{9,41},... | collective-permute-start | bytes 1376264 | tf_op jit(solution)/shard_map/ppermute | solution.py:82
  121.1 39.5 %collective-permute-start.6 = (bf16[3,144,1024]{2,1,0:T(8,128)(2,1)S(1)}, bf16[3,144,1024]{2,1,0:T(8,128)(2,1)S(1)}, u32[]{:S(2)}, u32[]{:S(2)}) collective-permute-start(bf16[3,144,1024]{2,1,0:T(8,128)(2,1)S(1)} %get-tuple-element.71), channel_id=1, source_target_pairs={{0,1},{1,2},{2,3},{3,4},{4,5},{5,6},{6,7},{7,8},{8,9},{9,10},{10,1... | collective-permute-start | bytes 2654216 | tf_op jit(solution)/shard_map/ppermute | solution.py:62
  122.0 7.9 %collective-permute-start.15 = (bf16[32,4096]{1,0:T(8,128)(2,1)S(1)}, bf16[32,4096]{1,0:T(8,128)(2,1)S(1)}, u32[]{:S(2)}, u32[]{:S(2)}) collective-permute-start(bf16[32,4096]{1,0:T(8,128)(2,1)S(1)} %get-tuple-element.83), channel_id=1, source_target_pairs={{0,16},{1,3},{2,18},{3,5},{4,20},{5,7},{6,22},{7,1},{8,24},{9,11},... | collective-permute-start | bytes 786440 | tf_op jit(solution)/shard_map/ppermute | solution.py:82
  122.3 10.1 %collective-permute-start.16 = (bf16[32,4096]{1,0:T(8,128)(2,1)S(1)}, bf16[32,4096]{1,0:T(8,128)(2,1)S(1)}, u32[]{:S(2)}, u32[]{:S(2)}) collective-permute-start(bf16[32,4096]{1,0:T(8,128)(2,1)S(1)} %get-tuple-element.84), channel_id=1, source_target_pairs={{0,48},{1,7},{2,50},{3,1},{4,52},{5,3},{6,54},{7,5},{8,56},{9,15},... | collective-permute-start | bytes 786440 | tf_op jit(solution)/shard_map/ppermute | solution.py:82
  125.7 8.6 %collective-permute-start.17 = (bf16[32,4096]{1,0:T(8,128)(2,1)S(1)}, bf16[32,4096]{1,0:T(8,128)(2,1)S(1)}, u32[]{:S(2)}, u32[]{:S(2)}) collective-permute-start(bf16[32,4096]{1,0:T(8,128)(2,1)S(1)} %get-tuple-element.85), channel_id=1, source_target_pairs={{0,32},{1,5},{2,34},{3,7},{4,36},{5,1},{6,38},{7,3},{8,40},{9,13},... | collective-permute-start | bytes 786440 | tf_op jit(solution)/shard_map/ppermute | solution.py:82
  127.1 33.5 %collective-permute-start.7 = (bf16[288,1024]{1,0:T(8,128)(2,1)S(1)}, bf16[288,1024]{1,0:T(8,128)(2,1)S(1)}, u32[]{:S(2)}, u32[]{:S(2)}) collective-permute-start(bf16[288,1024]{1,0:T(8,128)(2,1)S(1)} %get-tuple-element.72), channel_id=1, source_target_pairs={{0,16},{1,17},{2,18},{3,19},{4,20},{5,21},{6,22},{7,23},{8,24},{9,... | collective-permute-start | bytes 1769480 | tf_op jit(solution)/shard_map/ppermute | solution.py:62
  134.4 16.0 %collective-permute-start.18 = (f32[8,4096]{1,0:T(8,128)S(1)}, f32[8,4096]{1,0:T(8,128)S(1)}, u32[]{:S(2)}, u32[]{:S(2)}) collective-permute-start(f32[8,4096]{1,0:T(8,128)S(1)} %get-tuple-element.87), channel_id=1, source_target_pairs={{0,64},{1,65},{2,66},{3,67},{4,68},{5,69},{6,70},{7,71},{8,72},{9,... | collective-permute-start | bytes 393224 | tf_op jit(solution)/shard_map/ppermute | solution.py:82
  136.4 16.3 %collective-permute-start.19 = (f32[8,4096]{1,0:T(8,128)S(1)}, f32[8,4096]{1,0:T(8,128)S(1)}, u32[]{:S(2)}, u32[]{:S(2)}) collective-permute-start(f32[8,4096]{1,0:T(8,128)S(1)} %get-tuple-element.88), channel_id=1, source_target_pairs={{0,72},{1,73},{2,74},{3,75},{4,76},{5,77},{6,78},{7,79},{8,64},{9,... | collective-permute-start | bytes 393224 | tf_op jit(solution)/shard_map/ppermute | solution.py:82
  137.8 18.3 %collective-permute-start.20 = (f32[8,4096]{1,0:T(8,128)S(1)}, f32[8,4096]{1,0:T(8,128)S(1)}, u32[]{:S(2)}, u32[]{:S(2)}) collective-permute-start(f32[8,4096]{1,0:T(8,128)S(1)} %get-tuple-element.89), channel_id=1, source_target_pairs={{0,8},{1,9},{2,10},{3,11},{4,12},{5,13},{6,14},{7,15},{8,0},{9,1},... | collective-permute-start | bytes 393224 | tf_op jit(solution)/shard_map/ppermute | solution.py:82
  150.4 10.2 %collective-permute-start.8 = (bf16[80,1024]{1,0:T(8,128)(2,1)S(1)}, bf16[80,1024]{1,0:T(8,128)(2,1)S(1)}, u32[]{:S(2)}, u32[]{:S(2)}) collective-permute-start(bf16[80,1024]{1,0:T(8,128)(2,1)S(1)} %get-tuple-element.73), channel_id=1, source_target_pairs={{0,17},{1,18},{2,19},{3,20},{4,21},{5,22},{6,23},{7,24},{8,25},{9,... | collective-permute-start | bytes 491528 | tf_op jit(solution)/shard_map/ppermute | solution.py:62

commit v3 on v2

--- a/solution.py
+++ b/solution.py
@@ -221,22 +221,19 @@
         q_apart = apart(qw * jnp.asarray(0.125, bf16))
         d_apart = apart(dw)
         s = nt(kw, q_apart) + bias_ref[variant, 0].astype(f32)
+        dp = nt(vw, d_apart)
         e = jnp.exp(s - jnp.max(s, 0, keepdims=True))
         soft = e * (1.0 / jnp.sum(e, 0, keepdims=True))
         soft_b = soft.astype(bf16)
-        att_ref[rows] = gathered(tn(soft_b, vw)).astype(bf16)
-        dv = nn(soft_b, d_apart)
-        dp = nt(vw, d_apart)
         inner = jnp.sum(soft * dp, 0, keepdims=True)
         ds = (soft * (dp - inner)).astype(bf16)
-        dk = nn(ds, q_apart)
-        dq = gathered(tn(ds, kw)) * 0.125
-        gp_ref[0, rows] = dq.astype(bf16)
-        gp_ref[1, rows] = dk.astype(bf16)
-        gp_ref[2, rows] = dv.astype(bf16)
+        att_ref[rows] = gathered(tn(soft_b, vw)).astype(bf16)
+        gp_ref[2, rows] = nn(soft_b, d_apart).astype(bf16)
+        gp_ref[1, rows] = nn(ds, q_apart).astype(bf16)
+        gp_ref[0, rows] = (gathered(tn(ds, kw)) * 0.125).astype(bf16)
         return carry
 
-    lax.fori_loop(0, 6, window, 0)
+    lax.fori_loop(0, 6, window, 0, unroll=2)
 
 
 def split_rows(value, keep_ref, send_ref, at):

time: 163 us -> 154 us (0.945)
  Pallas kernels: 73.1 us -> 64.2 us
    pallas_call x2, Pallas kernels: 45.2 us -> 36.4 us  [some_quads(): pl.pallas_call(quads_kernel, grid_spec=pltpu.PrefetchScalarGridSpec(num_s...]
  transfers between devices with their start and end apart: 21 -> 21, of which waited for: 8 -> 8; matrix products, arithmetic and copies ran while one was open for 7% -> 8% of each run, Pallas kernels for 16% -> 16%
where the time goes in v3:
time: 154 us
  Pallas kernels  64.2 us (42%)
  starting transfers between devices  37.8 us (25%)
  waiting for transfers between devices  33.9 us (22%)
  local copies, waits for them, and re-layouts  13.8 us (9%)
  other arithmetic  3.29 us (2%)
    pallas_call x2, Pallas kernels, some_quads(): pl.pallas_call(quads_kernel, grid_spec=pltpu.PrefetchScalarGridSpec(num_s...  36.4 us
    ppermute x12, waiting for transfers between devices, ring_shift(): return lax.ppermute(value, ('lat', 'lon'), pairs)  29.9 us
    ppermute x12, starting transfers between devices, ring_shift(): return lax.ppermute(value, ('lat', 'lon'), pairs)  25.7 us
    pallas_call x1, Pallas kernels, epilogue(): pl.pallas_call(epilogue_kernel, grid=(3,), in_specs=[pl.BlockSpec((rows,...  13.5 us
    ppermute x6, starting transfers between devices, shift_grid(): return lax.ppermute(value, ('lat', 'lon'), pairs)  10.8 us
    another operation x3, local copies, waits for them, and re-layouts, per_device(): jnp.stack([table, jnp.where(differ, jnp.asarray(BLOCKED, bf16), table)])  5.32 us
    unnamed x27, local copies, waits for them, and re-layouts  5.03 us
    pallas_call x1, Pallas kernels, prologue(): pl.pallas_call(prologue_kernel, in_specs=[SMEM] + [VMEM] * 6, out_specs=[...  4.98 us
  transfers between devices with their start and end apart: 21, of which 8 were waited for; matrix products, arithmetic and copies ran while one was open for 8% of the time, Pallas kernels for 16%

profile of v3, /device:TPU:0, one launch (start us, length us, event | category | flops | bytes accessed | tf_op | source)
XLA Modules:
  0.0 153.9 jit_solution(14225167904096157461)
XLA Ops:
  0.6 1.5 copy-done.1
  2.1 1.5 copy-done.3
  3.6 1.3 strips.1
  4.9 5.6 %collective-permute-start = (bf16[432,1024]{1,0:T(8,128)(2,1)}, bf16[432,1024]{1,0:T(8,128)(2,1)}, u32[]{:S(2)}, u32[]{:S(2)}) collective-permute-start(bf16[432,1024]{1,0:T(8,128)(2,1)} %get-tuple-element.48), channel_id=1, source_target_pairs={{0,15},{1,0},{2,1},{3,2},{4,3},{5,4},{6,5},{7,6},{8,7},{9,8},{10,9... | collective-permute-start | bytes 2654216 | tf_op jit(solution)/shard_map/ppermute | solution.py:62
  10.5 3.5 %collective-permute-start.1 = (bf16[288,1024]{1,0:T(8,128)(2,1)}, bf16[288,1024]{1,0:T(8,128)(2,1)}, u32[]{:S(2)}, u32[]{:S(2)}) collective-permute-start(bf16[288,1024]{1,0:T(8,128)(2,1)} %get-tuple-element.49), channel_id=1, source_target_pairs={{0,112},{1,113},{2,114},{3,115},{4,116},{5,117},{6,118},{7,119},{8... | collective-permute-start | bytes 1769480 | tf_op jit(solution)/shard_map/ppermute | solution.py:62
  13.9 0.3 collective-permute-start.2
  14.3 2.1 %reshape.81 = bf16[4,4,144,144]{3,2,1,0:T(8,128)(2,1)S(1)} reshape(bf16[16,20736]{1,0:T(8,128)(2,1)S(1)} %copy-done.12) | data formatting | bytes 1327104 | tf_op jit(solution)/shard_map/reshape | solution.py:501
  16.4 1.3 copy.10
  17.7 0.8 stack.9
  18.5 0.7 broadcast_compare_fusion
  19.3 2.5 %broadcast_select_fusion = bf16[4,144,4,144]{3,2,1,0:T(4,128)(2,1)} fusion(pred[144,144]{1,0:T(8,128)(4,1)} %broadcast_compare_fusion, bf16[4,4,144,144]{2,1,3,0:T(4,128)(2,1)S(1)} %copy.10), kind=kLoop, calls=%fused_computation | loop fusion | flops 331776 | bytes 1347840 | tf_op jit(solution)/shard_map/jit(_where)/select_n | solution.py:504
  21.9 3.3 %stack.10 = bf16[1,4,144,576]{3,2,1,0:T(8,128)(2,1)} reshape(bf16[4,144,4,144]{3,2,1,0:T(4,128)(2,1)} %broadcast_select_fusion) | data formatting | bytes 1327104 | tf_op jit(solution)/shard_map/stack | solution.py:504
  25.2 1.2 constant_dynamic-update-slice_fusion.bias_ref
  26.5 1.5 copy-done.4
  28.0 5.0 %prologue.1 = (bf16[864,1024]{1,0:T(8,128)(2,1)S(1)}, bf16[864,1024]{1,0:T(8,128)(2,1)S(1)}, bf16[1024,864]{1,0:T(8,128)(2,1)S(1)}, bf16[864,1024]{1,0:T(8,128)(2,1)S(1)}) custom-call(s32[128]{0:T(128)S(1)} %fusion.2.place_ref, bf16[2,18,24,1024]{3,2,1,0:T(8,128)(2,1)S(1)} %copy-done.2, bf16[2,18,24,1024]{3,2,1,0:T(8,128)(2,1)S(1)} %copy-done.4, ...), custom_call_target="tpu_custom_call" | custom-call | flops 7000000000 | bytes 2100000 | tf_op jit(solution)/shard_map/prologue/pallas_call | solution.py:184
  33.0 27.2 %quads.2 = (bf16[864,768]{1,0:T(8,128)(2,1)S(1)}, bf16[3,864,768]{2,1,0:T(8,128)(2,1)}, bf16[512,2304]{1,0:T(8,128)(2,1)S(1)}, bf16[512,2304]{1,0:T(8,128)(2,1)}) custom-call(s32[1]{0:T(128)} %bitcast.pole_ref, bf16[864,1024]{1,0:T(8,128)(2,1)S(1)} %get-tuple-element.51.n_ref, bf16[1024,864]{1,0:T(8,128)(2,1)S(1)} %get-tuple-element.52.nt_ref, ...), custom_call_target="tpu_custom_call" | custom-call | flops 32999999488 | bytes 9900000 | tf_op jit(solution)/shard_map/quads/pallas_call | solution.py:279
  60.2 0.6 collective-permute-start.3
  60.8 9.2 %quads.3 = (bf16[864,256]{1,0:T(8,128)(2,1)S(1)}, bf16[3,864,256]{2,1,0:T(8,128)(2,1)S(1)}, bf16[512,768]{1,0:T(8,128)(2,1)S(1)}, bf16[512,768]{1,0:T(8,128)(2,1)S(1)}) custom-call(s32[1]{0:T(128)} %bitcast.pole_ref, bf16[864,1024]{1,0:T(8,128)(2,1)S(1)} %get-tuple-element.51.n_ref, bf16[1024,864]{1,0:T(8,128)(2,1)S(1)} %get-tuple-element.52.nt_ref, ...), custom_call_target="tpu_custom_call" | custom-call | flops 11000000512 | bytes 3300000 | tf_op jit(solution)/shard_map/quads/pallas_call | solution.py:279
  70.0 0.5 core_sum.2
  70.6 0.5 copy-done.8
  71.1 3.4 %out_grads.1 = (bf16[512,1024]{1,0:T(8,128)(2,1)S(1)}, bf16[512,1024]{1,0:T(8,128)(2,1)S(1)}) custom-call(s32[128]{0:T(128)S(1)} %fusion.2.place_ref, bf16[864,768]{1,0:T(8,128)(2,1)S(1)} %get-tuple-element.54.before_ref.att_ref, bf16[864,256]{1,0:T(8,128)(2,1)S(1)} %get-tuple-element.65.after_ref.att2_ref, bf16[864,1024]{1,0:T(8,128)(2,1)S(1)} %get-tuple-element.53.gw_ref), custom_call_target="tpu_custom_call" | custom-call | flops 7000000000 | bytes 2100000 | tf_op jit(solution)/shard_map/out_grads/pallas_call | solution.py:304
  74.5 0.6 collective-permute-start.5
  75.0 0.1 collective-permute-start.4
  75.1 9.9 %collective-permute-start.10 = (bf16[128,2304]{1,0:T(8,128)(2,1)S(1)}, bf16[128,2304]{1,0:T(8,128)(2,1)S(1)}, u32[]{:S(2)}, u32[]{:S(2)}) collective-permute-start(bf16[128,2304]{1,0:T(8,128)(2,1)S(1)} %get-tuple-element.77), channel_id=1, source_target_pairs={{0,6},{1,49},{2,0},{3,51},{4,2},{5,53},{6,4},{7,55},{8,14},{9,57},... | collective-permute-start | bytes 1769480 | tf_op jit(solution)/shard_map/ppermute | solution.py:82
  85.0 1.5 collective-permute-start.11
  86.5 0.4 core_sum.3
  87.0 2.7 %collective-permute-start.12 = (bf16[128,1792]{1,0:T(8,128)(2,1)S(1)}, bf16[128,1792]{1,0:T(8,128)(2,1)S(1)}, u32[]{:S(2)}, u32[]{:S(2)}) collective-permute-start(bf16[128,1792]{1,0:T(8,128)(2,1)S(1)} %get-tuple-element.64), channel_id=1, source_target_pairs={{0,2},{1,17},{2,4},{3,19},{4,6},{5,21},{6,0},{7,23},{8,10},{9,25},... | collective-permute-start | bytes 1376264 | tf_op jit(solution)/shard_map/ppermute | solution.py:82
  89.7 0.6 collective-permute-start.13
  90.3 8.5 %collective-permute-done.10.refs_2_ = bf16[128,2304]{1,0:T(8,128)(2,1)S(1)} collective-permute-done((bf16[128,2304]{1,0:T(8,128)(2,1)S(1)}, bf16[128,2304]{1,0:T(8,128)(2,1)S(1)}, u32[]{:S(2)}, u32[]{:S(2)}) %collective-permute-start.10) | collective-permute-done | bytes 589856 | tf_op jit(solution)/shard_map/ppermute | solution.py:82
  98.8 13.5 %epilogue.1 = (bf16[2,18,24,1024]{3,2,1,0:T(8,128)(2,1)S(1)}, bf16[2,18,24,1024]{3,2,1,0:T(8,128)(2,1)S(1)}, bf16[3,144,1024]{2,1,0:T(8,128)(2,1)S(1)}, bf16[288...) custom-call(bf16[864,768]{1,0:T(8,128)(2,1)S(1)} %copy-done.11, bf16[864,256]{1,0:T(8,128)(2,1)S(1)} %get-tuple-element.65.after_ref.att2_ref, ...), custom_call_target="tpu_custom_call" | custom-call | flops 16000000000 | bytes 4800000 | tf_op jit(solution)/shard_map/epilogue/pallas_call | solution.py:358
  112.5 0.5 ring_sum.2
  113.0 0.2 collective-permute-start.15
  113.2 3.4 %collective-permute-start.16 = (bf16[32,4096]{1,0:T(8,128)(2,1)S(1)}, bf16[32,4096]{1,0:T(8,128)(2,1)S(1)}, u32[]{:S(2)}, u32[]{:S(2)}) collective-permute-start(bf16[32,4096]{1,0:T(8,128)(2,1)S(1)} %get-tuple-element.84), channel_id=1, source_target_pairs={{0,48},{1,7},{2,50},{3,1},{4,52},{5,3},{6,54},{7,5},{8,56},{9,15},... | collective-permute-start | bytes 786440 | tf_op jit(solution)/shard_map/ppermute | solution.py:82
  116.6 1.4 collective-permute-start.17
  118.0 1.4 collective-permute-start.7
  119.4 1.5 collective-permute-done.15.refs_1_
  120.9 2.5 %collective-permute-done.16.refs_2_ = bf16[32,4096]{1,0:T(8,128)(2,1)S(1)} collective-permute-done((bf16[32,4096]{1,0:T(8,128)(2,1)S(1)}, bf16[32,4096]{1,0:T(8,128)(2,1)S(1)}, u32[]{:S(2)}, u32[]{:S(2)}) %collective-permute-start.16) | collective-permute-done | bytes 262176 | tf_op jit(solution)/shard_map/ppermute | solution.py:82
  123.4 1.9 %collective-permute-done.17.refs_3_ = bf16[32,4096]{1,0:T(8,128)(2,1)S(1)} collective-permute-done((bf16[32,4096]{1,0:T(8,128)(2,1)S(1)}, bf16[32,4096]{1,0:T(8,128)(2,1)S(1)}, u32[]{:S(2)}, u32[]{:S(2)}) %collective-permute-start.17) | collective-permute-done | bytes 262176 | tf_op jit(solution)/shard_map/ppermute | solution.py:82
  125.3 0.1 ring_sum.3
  125.4 2.0 %collective-permute-start.18 = (f32[8,4096]{1,0:T(8,128)S(1)}, f32[8,4096]{1,0:T(8,128)S(1)}, u32[]{:S(2)}, u32[]{:S(2)}) collective-permute-start(f32[8,4096]{1,0:T(8,128)S(1)} %get-tuple-element.87), channel_id=1, source_target_pairs={{0,64},{1,65},{2,66},{3,67},{4,68},{5,69},{6,70},{7,71},{8,72},{9,... | collective-permute-start | bytes 393224 | tf_op jit(solution)/shard_map/ppermute | solution.py:82
  127.4 1.3 collective-permute-start.19
  128.7 2.7 %collective-permute-start.20 = (f32[8,4096]{1,0:T(8,128)S(1)}, f32[8,4096]{1,0:T(8,128)S(1)}, u32[]{:S(2)}, u32[]{:S(2)}) collective-permute-start(f32[8,4096]{1,0:T(8,128)S(1)} %get-tuple-element.89), channel_id=1, source_target_pairs={{0,8},{1,9},{2,10},{3,11},{4,12},{5,13},{6,14},{7,15},{8,0},{9,1},... | collective-permute-start | bytes 393224 | tf_op jit(solution)/shard_map/ppermute | solution.py:82
  131.4 10.0 %collective-permute-done.18.b = f32[8,4096]{1,0:T(8,128)S(1)} collective-permute-done((f32[8,4096]{1,0:T(8,128)S(1)}, f32[8,4096]{1,0:T(8,128)S(1)}, u32[]{:S(2)}, u32[]{:S(2)}) %collective-permute-start.18) | collective-permute-done | bytes 131104 | tf_op jit(solution)/shard_map/ppermute | solution.py:82
  141.4 2.3 %collective-permute-done.19.c = f32[8,4096]{1,0:T(8,128)S(1)} collective-permute-done((f32[8,4096]{1,0:T(8,128)S(1)}, f32[8,4096]{1,0:T(8,128)S(1)}, u32[]{:S(2)}, u32[]{:S(2)}) %collective-permute-start.19) | collective-permute-done | bytes 131104 | tf_op jit(solution)/shard_map/ppermute | solution.py:82
  143.7 3.3 %collective-permute-done.20.d = f32[8,4096]{1,0:T(8,128)S(1)} collective-permute-done((f32[8,4096]{1,0:T(8,128)S(1)}, f32[8,4096]{1,0:T(8,128)S(1)}, u32[]{:S(2)}, u32[]{:S(2)}) %collective-permute-start.20) | collective-permute-done | bytes 131104 | tf_op jit(solution)/shard_map/ppermute | solution.py:82
  146.9 0.7 finish.1
  147.6 3.9 %collective-permute-done.8.corner_ref = bf16[80,1024]{1,0:T(8,128)(2,1)S(1)} collective-permute-done((bf16[80,1024]{1,0:T(8,128)(2,1)S(1)}, bf16[80,1024]{1,0:T(8,128)(2,1)S(1)}, u32[]{:S(2)}, u32[]{:S(2)}) %collective-permute-start.8) | collective-permute-done | bytes 163872 | tf_op jit(solution)/shard_map/ppermute | solution.py:62
  151.6 2.4 %restore.1 = (bf16[2,18,24,1024]{3,2,1,0:T(8,128)(2,1)}, bf16[2,18,24,1024]{3,2,1,0:T(8,128)(2,1)}) custom-call(bf16[2,18,24,1024]{3,2,1,0:T(8,128)(2,1)S(1)} %get-tuple-element.69.out_ref, bf16[2,18,24,1024]{3,2,1,0:T(8,128)(2,1)S(1)} %get-tuple-element.70.grad_ref, bf16[3,144,1024]{2,1,0:T(8,128)(2,1)S(1)} %collective-permute-done.6.cols_ref, ...), custom_call_target="tpu_custom_call" | custom-call | flops 5000000000 | bytes 1500000 | tf_op jit(solution)/shard_map/restore/pallas_call | solution.py:404
  (42 shorter events, 0.3 us)
Async XLA Ops:
  0.6 1.5 copy-start.1
  2.1 1.5 copy-start.3
  3.6 10.7 %copy-start.12 = (bf16[16,20736]{1,0:T(8,128)(2,1)S(1)}, bf16[16,20736]{1,0:T(8,128)(2,1)}, u32[]{:S(2)}) copy-start(bf16[16,20736]{1,0:T(8,128)(2,1)} %param.11) | copy-start | bytes 1990660
  4.9 21.6 %collective-permute-start = (bf16[432,1024]{1,0:T(8,128)(2,1)}, bf16[432,1024]{1,0:T(8,128)(2,1)}, u32[]{:S(2)}, u32[]{:S(2)}) collective-permute-start(bf16[432,1024]{1,0:T(8,128)(2,1)} %get-tuple-element.48), channel_id=1, source_target_pairs={{0,15},{1,0},{2,1},{3,2},{4,3},{5,4},{6,5},{7,6},{8,7},{9,8},{10,9... | collective-permute-start | bytes 2654216 | tf_op jit(solution)/shard_map/ppermute | solution.py:62
  10.5 16.0 %collective-permute-start.1 = (bf16[288,1024]{1,0:T(8,128)(2,1)}, bf16[288,1024]{1,0:T(8,128)(2,1)}, u32[]{:S(2)}, u32[]{:S(2)}) collective-permute-start(bf16[288,1024]{1,0:T(8,128)(2,1)} %get-tuple-element.49), channel_id=1, source_target_pairs={{0,112},{1,113},{2,114},{3,115},{4,116},{5,117},{6,118},{7,119},{8... | collective-permute-start | bytes 1769480 | tf_op jit(solution)/shard_map/ppermute | solution.py:62
  13.9 12.5 %collective-permute-start.2 = (bf16[80,1024]{1,0:T(8,128)(2,1)}, bf16[80,1024]{1,0:T(8,128)(2,1)S(1)}, u32[]{:S(2)}, u32[]{:S(2)}) collective-permute-start(bf16[80,1024]{1,0:T(8,128)(2,1)} %get-tuple-element.50), channel_id=1, source_target_pairs={{0,127},{1,112},{2,113},{3,114},{4,115},{5,116},{6,117},{7,118},{8... | collective-permute-start | bytes 491528 | tf_op jit(solution)/shard_map/ppermute | solution.py:62
  21.9 4.6 %copy-start.2 = (bf16[2,18,24,1024]{3,2,1,0:T(8,128)(2,1)S(1)}, bf16[2,18,24,1024]{3,2,1,0:T(8,128)(2,1)}, u32[]{:S(2)}) copy-start(bf16[2,18,24,1024]{3,2,1,0:T(8,128)(2,1)} %lat_ref.3) | copy-start | bytes 5308420
  21.9 4.6 %copy-start.5 = (f32[1024]{0:T(1024)S(1)}, f32[1024]{0:T(1024)}, u32[]{:S(2)}) copy-start(f32[1024]{0:T(1024)} %param.10) | copy-start | bytes 12292
  26.5 1.5 copy-start.4
  28.0 5.0 %copy-start = (bf16[1024,1024]{1,0:T(8,128)(2,1)S(1)}, bf16[1024,1024]{1,0:T(8,128)(2,1)}, u32[]{:S(2)}) copy-start(bf16[1024,1024]{1,0:T(8,128)(2,1)} %wo_ref.5) | copy-start | bytes 6291460
  33.0 38.1 %copy-start.6 = (bf16[864,1024]{1,0:T(8,128)(2,1)}, bf16[864,1024]{1,0:T(8,128)(2,1)S(1)}, u32[]{:S(2)}) copy-start(bf16[864,1024]{1,0:T(8,128)(2,1)S(1)} %get-tuple-element.53.gw_ref) | copy-start | bytes 5308420
  60.2 10.9 %copy-start.10 = (bf16[864,768]{1,0:T(8,128)(2,1)}, bf16[864,768]{1,0:T(8,128)(2,1)S(1)}, u32[]{:S(2)}) copy-start(bf16[864,768]{1,0:T(8,128)(2,1)S(1)} %get-tuple-element.54.before_ref.att_ref) | copy-start | bytes 3981316
  60.2 9.8 %collective-permute-start.3 = (bf16[512,2304]{1,0:T(8,128)(2,1)}, bf16[512,2304]{1,0:T(8,128)(2,1)S(1)}, u32[]{:S(2)}, u32[]{:S(2)}) collective-permute-start(bf16[512,2304]{1,0:T(8,128)(2,1)} %get-tuple-element.57), channel_id=1, source_target_pairs={{0,1},{1,0},{2,3},{3,2},{4,5},{5,4},{6,7},{7,6},{8,9},{9,8},{10,11... | collective-permute-start | bytes 7077896 | tf_op jit(solution)/shard_map/ppermute | solution.py:54
  70.0 1.1 copy-start.8
  74.5 12.0 %collective-permute-start.5 = (bf16[512,1024]{1,0:T(8,128)(2,1)S(1)}, bf16[512,1024]{1,0:T(8,128)(2,1)S(1)}, u32[]{:S(2)}, u32[]{:S(2)}) collective-permute-start(bf16[512,1024]{1,0:T(8,128)(2,1)S(1)} %get-tuple-element.63), channel_id=1, source_target_pairs={{0,1},{1,0},{2,3},{3,2},{4,5},{5,4},{6,7},{7,6},{8,9},{9,8},{10,11... | collective-permute-start | bytes 3145736 | tf_op jit(solution)/shard_map/ppermute | solution.py:54
  75.0 11.5 %collective-permute-start.4 = (bf16[512,768]{1,0:T(8,128)(2,1)S(1)}, bf16[512,768]{1,0:T(8,128)(2,1)S(1)}, u32[]{:S(2)}, u32[]{:S(2)}) collective-permute-start(bf16[512,768]{1,0:T(8,128)(2,1)S(1)} %get-tuple-element.61), channel_id=1, source_target_pairs={{0,1},{1,0},{2,3},{3,2},{4,5},{5,4},{6,7},{7,6},{8,9},{9,8},{10,11... | collective-permute-start | bytes 2359304 | tf_op jit(solution)/shard_map/ppermute | solution.py:54
  75.1 23.6 %collective-permute-start.10 = (bf16[128,2304]{1,0:T(8,128)(2,1)S(1)}, bf16[128,2304]{1,0:T(8,128)(2,1)S(1)}, u32[]{:S(2)}, u32[]{:S(2)}) collective-permute-start(bf16[128,2304]{1,0:T(8,128)(2,1)S(1)} %get-tuple-element.77), channel_id=1, source_target_pairs={{0,6},{1,49},{2,0},{3,51},{4,2},{5,53},{6,4},{7,55},{8,14},{9,57},... | collective-permute-start | bytes 1769480 | tf_op jit(solution)/shard_map/ppermute | solution.py:82
  85.0 27.4 %collective-permute-start.9 = (bf16[128,2304]{1,0:T(8,128)(2,1)S(1)}, bf16[128,2304]{1,0:T(8,128)(2,1)S(1)}, u32[]{:S(2)}, u32[]{:S(2)}) collective-permute-start(bf16[128,2304]{1,0:T(8,128)(2,1)S(1)} %get-tuple-element.58), channel_id=1, source_target_pairs={{0,2},{1,17},{2,4},{3,19},{4,6},{5,21},{6,0},{7,23},{8,10},{9,25},... | collective-permute-start | bytes 1769480 | tf_op jit(solution)/shard_map/ppermute | solution.py:82
  85.0 27.3 %collective-permute-start.11 = (bf16[128,2304]{1,0:T(8,128)(2,1)S(1)}, bf16[128,2304]{1,0:T(8,128)(2,1)S(1)}, u32[]{:S(2)}, u32[]{:S(2)}) collective-permute-start(bf16[128,2304]{1,0:T(8,128)(2,1)S(1)} %get-tuple-element.78), channel_id=1, source_target_pairs={{0,4},{1,33},{2,6},{3,35},{4,0},{5,37},{6,2},{7,39},{8,12},{9,41},... | collective-permute-start | bytes 1769480 | tf_op jit(solution)/shard_map/ppermute | solution.py:82
  86.5 12.3 %copy-start.7 = (bf16[864,1024]{1,0:T(8,128)(2,1)S(1)}, bf16[864,1024]{1,0:T(8,128)(2,1)}, u32[]{:S(2)}) copy-start(bf16[864,1024]{1,0:T(8,128)(2,1)} %copy-done.6) | copy-start | bytes 5308420
  86.5 12.3 %copy-start.9 = (bf16[3,864,256]{2,1,0:T(8,128)(2,1)S(1)}, bf16[3,864,256]{2,1,0:T(8,128)(2,1)}, u32[]{:S(2)}) copy-start(bf16[3,864,256]{2,1,0:T(8,128)(2,1)} %copy-done.8) | copy-start | bytes 3981316
  86.5 12.2 %copy-start.11 = (bf16[864,768]{1,0:T(8,128)(2,1)S(1)}, bf16[864,768]{1,0:T(8,128)(2,1)}, u32[]{:S(2)}) copy-start(bf16[864,768]{1,0:T(8,128)(2,1)} %copy-done.10) | copy-start | bytes 3981316
  87.0 25.5 %collective-permute-start.12 = (bf16[128,1792]{1,0:T(8,128)(2,1)S(1)}, bf16[128,1792]{1,0:T(8,128)(2,1)S(1)}, u32[]{:S(2)}, u32[]{:S(2)}) collective-permute-start(bf16[128,1792]{1,0:T(8,128)(2,1)S(1)} %get-tuple-element.64), channel_id=1, source_target_pairs={{0,2},{1,17},{2,4},{3,19},{4,6},{5,21},{6,0},{7,23},{8,10},{9,25},... | collective-permute-start | bytes 1376264 | tf_op jit(solution)/shard_map/ppermute | solution.py:82
  89.7 22.8 %collective-permute-start.13 = (bf16[128,1792]{1,0:T(8,128)(2,1)S(1)}, bf16[128,1792]{1,0:T(8,128)(2,1)S(1)}, u32[]{:S(2)}, u32[]{:S(2)}) collective-permute-start(bf16[128,1792]{1,0:T(8,128)(2,1)S(1)} %get-tuple-element.80), channel_id=1, source_target_pairs={{0,6},{1,49},{2,0},{3,51},{4,2},{5,53},{6,4},{7,55},{8,14},{9,57},... | collective-permute-start | bytes 1376264 | tf_op jit(solution)/shard_map/ppermute | solution.py:82
  98.8 13.7 %collective-permute-start.14 = (bf16[128,1792]{1,0:T(8,128)(2,1)S(1)}, bf16[128,1792]{1,0:T(8,128)(2,1)S(1)}, u32[]{:S(2)}, u32[]{:S(2)}) collective-permute-start(bf16[128,1792]{1,0:T(8,128)(2,1)S(1)} %get-tuple-element.81), channel_id=1, source_target_pairs={{0,4},{1,33},{2,6},{3,35},{4,0},{5,37},{6,2},{7,39},{8,12},{9,41},... | collective-permute-start | bytes 1376264 | tf_op jit(solution)/shard_map/ppermute | solution.py:82
  112.3 39.2 %collective-permute-start.6 = (bf16[3,144,1024]{2,1,0:T(8,128)(2,1)S(1)}, bf16[3,144,1024]{2,1,0:T(8,128)(2,1)S(1)}, u32[]{:S(2)}, u32[]{:S(2)}) collective-permute-start(bf16[3,144,1024]{2,1,0:T(8,128)(2,1)S(1)} %get-tuple-element.71), channel_id=1, source_target_pairs={{0,1},{1,2},{2,3},{3,4},{4,5},{5,6},{6,7},{7,8},{8,9},{9,10},{10,1... | collective-permute-start | bytes 2654216 | tf_op jit(solution)/shard_map/ppermute | solution.py:62
  113.0 7.9 %collective-permute-start.15 = (bf16[32,4096]{1,0:T(8,128)(2,1)S(1)}, bf16[32,4096]{1,0:T(8,128)(2,1)S(1)}, u32[]{:S(2)}, u32[]{:S(2)}) collective-permute-start(bf16[32,4096]{1,0:T(8,128)(2,1)S(1)} %get-tuple-element.83), channel_id=1, source_target_pairs={{0,16},{1,3},{2,18},{3,5},{4,20},{5,7},{6,22},{7,1},{8,24},{9,11},... | collective-permute-start | bytes 786440 | tf_op jit(solution)/shard_map/ppermute | solution.py:82
  113.2 10.1 %collective-permute-start.16 = (bf16[32,4096]{1,0:T(8,128)(2,1)S(1)}, bf16[32,4096]{1,0:T(8,128)(2,1)S(1)}, u32[]{:S(2)}, u32[]{:S(2)}) collective-permute-start(bf16[32,4096]{1,0:T(8,128)(2,1)S(1)} %get-tuple-element.84), channel_id=1, source_target_pairs={{0,48},{1,7},{2,50},{3,1},{4,52},{5,3},{6,54},{7,5},{8,56},{9,15},... | collective-permute-start | bytes 786440 | tf_op jit(solution)/shard_map/ppermute | solution.py:82
  116.6 8.6 %collective-permute-start.17 = (bf16[32,4096]{1,0:T(8,128)(2,1)S(1)}, bf16[32,4096]{1,0:T(8,128)(2,1)S(1)}, u32[]{:S(2)}, u32[]{:S(2)}) collective-permute-start(bf16[32,4096]{1,0:T(8,128)(2,1)S(1)} %get-tuple-element.85), channel_id=1, source_target_pairs={{0,32},{1,5},{2,34},{3,7},{4,36},{5,1},{6,38},{7,3},{8,40},{9,13},... | collective-permute-start | bytes 786440 | tf_op jit(solution)/shard_map/ppermute | solution.py:82
  118.0 33.5 %collective-permute-start.7 = (bf16[288,1024]{1,0:T(8,128)(2,1)S(1)}, bf16[288,1024]{1,0:T(8,128)(2,1)S(1)}, u32[]{:S(2)}, u32[]{:S(2)}) collective-permute-start(bf16[288,1024]{1,0:T(8,128)(2,1)S(1)} %get-tuple-element.72), channel_id=1, source_target_pairs={{0,16},{1,17},{2,18},{3,19},{4,20},{5,21},{6,22},{7,23},{8,24},{9,... | collective-permute-start | bytes 1769480 | tf_op jit(solution)/shard_map/ppermute | solution.py:62
  125.4 16.0 %collective-permute-start.18 = (f32[8,4096]{1,0:T(8,128)S(1)}, f32[8,4096]{1,0:T(8,128)S(1)}, u32[]{:S(2)}, u32[]{:S(2)}) collective-permute-start(f32[8,4096]{1,0:T(8,128)S(1)} %get-tuple-element.87), channel_id=1, source_target_pairs={{0,64},{1,65},{2,66},{3,67},{4,68},{5,69},{6,70},{7,71},{8,72},{9,... | collective-permute-start | bytes 393224 | tf_op jit(solution)/shard_map/ppermute | solution.py:82
  127.4 16.3 %collective-permute-start.19 = (f32[8,4096]{1,0:T(8,128)S(1)}, f32[8,4096]{1,0:T(8,128)S(1)}, u32[]{:S(2)}, u32[]{:S(2)}) collective-permute-start(f32[8,4096]{1,0:T(8,128)S(1)} %get-tuple-element.88), channel_id=1, source_target_pairs={{0,72},{1,73},{2,74},{3,75},{4,76},{5,77},{6,78},{7,79},{8,64},{9,... | collective-permute-start | bytes 393224 | tf_op jit(solution)/shard_map/ppermute | solution.py:82
  128.7 18.3 %collective-permute-start.20 = (f32[8,4096]{1,0:T(8,128)S(1)}, f32[8,4096]{1,0:T(8,128)S(1)}, u32[]{:S(2)}, u32[]{:S(2)}) collective-permute-start(f32[8,4096]{1,0:T(8,128)S(1)} %get-tuple-element.89), channel_id=1, source_target_pairs={{0,8},{1,9},{2,10},{3,11},{4,12},{5,13},{6,14},{7,15},{8,0},{9,1},... | collective-permute-start | bytes 393224 | tf_op jit(solution)/shard_map/ppermute | solution.py:82
  141.4 10.2 %collective-permute-start.8 = (bf16[80,1024]{1,0:T(8,128)(2,1)S(1)}, bf16[80,1024]{1,0:T(8,128)(2,1)S(1)}, u32[]{:S(2)}, u32[]{:S(2)}) collective-permute-start(bf16[80,1024]{1,0:T(8,128)(2,1)S(1)} %get-tuple-element.73), channel_id=1, source_target_pairs={{0,17},{1,18},{2,19},{3,20},{4,21},{5,22},{6,23},{7,24},{8,25},{9,... | collective-permute-start | bytes 491528 | tf_op jit(solution)/shard_map/ppermute | solution.py:62

commit v4 on v3

--- a/solution.py
+++ b/solution.py
@@ -511,21 +511,18 @@
     got = shift(send, "c", 1)
     att2, gp2, keep2, send2 = some_quads(FIRST, 1, pole, normed, normed_t, gw, qkv_weight, out_weight, bias)
     got2 = shift(send2, "c", 1)
-    pieces = core_sum(keep, got)
+    keep3, send3 = out_grads(place, att, att2, gw)
+    got3 = shift(send3, "c", 1)
+    pieces = core_sum(keep, got, keep2, got2, keep3, got3)
     moved = ring(pieces, 0)
     att2, _ = lax.optimization_barrier((att2, pieces[1]))
-    keep3, send3 = out_grads(place, att, att2, gw)
-    got3 = shift(send3, "c", 1)
-    pieces2 = core_sum(keep2, got2, keep3, got3)
-    moved2 = ring(pieces2, 0)
-    att2, _ = lax.optimization_barrier((att2, pieces2[1]))
     out_tile, grad_tile, cols, rows, corner = epilogue(
         att, att2, gp, gp2, out_weight, qkv_weight, xw, gw, gain
     )
     cols = shift_grid(cols, 0, 1)
     rows = shift_grid(rows, 1, 0)
     corner = shift_grid(corner, 1, 1)
-    pieces = ring_sum(bf16, [pieces[0]] + moved, [pieces2[0]] + moved2)
+    pieces = ring_sum(bf16, [pieces[0]] + moved)
     pieces = ring_sum(f32, [pieces[0]] + ring(pieces, 1))
     updated, grad_input = restored(out_tile, grad_tile, cols, rows, corner)
     qkv_grad, out_grad = finish(pieces[0], ring(pieces, 2))

time: 154 us -> 153 us (level)
  waiting for transfers between devices: 33.9 us -> 30.4 us
  starting transfers between devices: 37.8 us -> 39.4 us
    ppermute x12 -> x9, waiting for transfers between devices: 29.9 us -> 25.1 us  [ring_shift(): return lax.ppermute(value, ('lat', 'lon'), pairs)]
    ppermute x3, waiting for transfers between devices: 0.01 us -> 3.28 us  [shift(): return lax.ppermute(value, ('lat', 'lon'), pairs)]
    ppermute x12 -> x9, starting transfers between devices: 25.7 us -> 27.9 us  [ring_shift(): return lax.ppermute(value, ('lat', 'lon'), pairs)]
    ppermute x6, waiting for transfers between devices: 3.94 us -> 2.08 us  [shift_grid(): return lax.ppermute(value, ('lat', 'lon'), pairs)]
    unnamed x27 -> x25, local copies, waits for them, and re-layouts: 5.03 us -> 4.52 us
  transfers between devices with their start and end apart: 21 -> 18, of which waited for: 8 -> 8; matrix products, arithmetic and copies ran while one was open for 8% -> 8% of each run, Pallas kernels for 16% -> 19%
where the time goes in v4:
time: 153 us; the launch traced here: 152 us
  Pallas kernels  64.7 us (42%)
  starting transfers between devices  39.4 us (26%)
  waiting for transfers between devices  30.4 us (20%)
  local copies, waits for them, and re-layouts  13.2 us (9%)
  other arithmetic  3.79 us (2%)
    pallas_call x2, Pallas kernels, some_quads(): pl.pallas_call(quads_kernel, grid_spec=pltpu.PrefetchScalarGridSpec(num_s...  36.9 us
    ppermute x9, starting transfers between devices, ring_shift(): return lax.ppermute(value, ('lat', 'lon'), pairs)  27.9 us
    ppermute x9, waiting for transfers between devices, ring_shift(): return lax.ppermute(value, ('lat', 'lon'), pairs)  25.1 us
    pallas_call x1, Pallas kernels, epilogue(): pl.pallas_call(epilogue_kernel, grid=(3,), in_specs=[pl.BlockSpec((rows,...  13.5 us
    ppermute x6, starting transfers between devices, shift_grid(): return lax.ppermute(value, ('lat', 'lon'), pairs)  10.8 us
    another operation x3, local copies, waits for them, and re-layouts, per_device(): jnp.stack([table, jnp.where(differ, jnp.asarray(BLOCKED, bf16), table)])  5.28 us
    pallas_call x1, Pallas kernels, prologue(): pl.pallas_call(prologue_kernel, in_specs=[SMEM] + [VMEM] * 6, out_specs=[...  4.98 us
    unnamed x25, local copies, waits for them, and re-layouts  4.52 us
  transfers between devices with their start and end apart: 18, of which 8 were waited for; matrix products, arithmetic and copies ran while one was open for 8% of the time, Pallas kernels for 19%

profile of v4, /device:TPU:0, one launch (start us, length us, event | category | flops | bytes accessed | tf_op | source)
XLA Modules:
  0.0 152.5 jit_solution(1821899388187637416)
XLA Ops:
  0.6 0.0 copy-start.1
  0.6 1.5 copy-done.1
  2.1 1.5 copy-done.3
  3.6 1.3 strips.1
  4.9 8.2 %collective-permute-start.2 = (bf16[80,1024]{1,0:T(8,128)(2,1)}, bf16[80,1024]{1,0:T(8,128)(2,1)S(1)}, u32[]{:S(2)}, u32[]{:S(2)}) collective-permute-start(bf16[80,1024]{1,0:T(8,128)(2,1)} %get-tuple-element.45), channel_id=1, source_target_pairs={{0,127},{1,112},{2,113},{3,114},{4,115},{5,116},{6,117},{7,118},{8... | collective-permute-start | bytes 491528 | tf_op jit(solution)/shard_map/ppermute | solution.py:62
  13.1 1.0 collective-permute-start.1
  14.1 1.2 collective-permute-start
  15.3 0.5 fusion
  15.8 2.1 %reshape.81 = bf16[4,4,144,144]{3,2,1,0:T(8,128)(2,1)S(1)} reshape(bf16[16,20736]{1,0:T(8,128)(2,1)S(1)} %copy-done.10) | data formatting | bytes 1327104 | tf_op jit(solution)/shard_map/reshape | solution.py:501
  18.0 1.3 copy.10
  19.3 0.8 stack.9
  20.1 0.7 broadcast_compare_fusion
  20.8 0.1 constant_dynamic-update-slice_fusion.1
  20.9 2.5 %broadcast_select_fusion = bf16[4,144,4,144]{3,2,1,0:T(4,128)(2,1)} fusion(pred[144,144]{1,0:T(8,128)(4,1)} %broadcast_compare_fusion, bf16[4,4,144,144]{2,1,3,0:T(4,128)(2,1)S(1)} %copy.10), kind=kLoop, calls=%fused_computation | loop fusion | flops 331776 | bytes 1347840 | tf_op jit(solution)/shard_map/jit(_where)/select_n | solution.py:504
  23.5 3.3 %stack.10 = bf16[1,4,144,576]{3,2,1,0:T(8,128)(2,1)} reshape(bf16[4,144,4,144]{3,2,1,0:T(4,128)(2,1)} %broadcast_select_fusion) | data formatting | bytes 1327104 | tf_op jit(solution)/shard_map/stack | solution.py:504
  26.8 1.2 constant_dynamic-update-slice_fusion.bias_ref
  28.1 1.5 copy-done.4
  29.5 5.0 %prologue.1 = (bf16[864,1024]{1,0:T(8,128)(2,1)S(1)}, bf16[864,1024]{1,0:T(8,128)(2,1)S(1)}, bf16[1024,864]{1,0:T(8,128)(2,1)S(1)}, bf16[864,1024]{1,0:T(8,128)(2,1)S(1)}) custom-call(s32[128]{0:T(128)S(1)} %fusion.2.place_ref, bf16[2,18,24,1024]{3,2,1,0:T(8,128)(2,1)S(1)} %copy-done.2, bf16[2,18,24,1024]{3,2,1,0:T(8,128)(2,1)S(1)} %copy-done.4, ...), custom_call_target="tpu_custom_call" | custom-call | flops 7000000000 | bytes 2100000 | tf_op jit(solution)/shard_map/prologue/pallas_call | solution.py:184
  34.5 27.2 %quads.2 = (bf16[864,768]{1,0:T(8,128)(2,1)S(1)}, bf16[3,864,768]{2,1,0:T(8,128)(2,1)}, bf16[512,2304]{1,0:T(8,128)(2,1)S(1)}, bf16[512,2304]{1,0:T(8,128)(2,1)}) custom-call(s32[1]{0:T(128)} %bitcast.pole_ref, bf16[864,1024]{1,0:T(8,128)(2,1)S(1)} %get-tuple-element.46.n_ref, bf16[1024,864]{1,0:T(8,128)(2,1)S(1)} %get-tuple-element.47.nt_ref, ...), custom_call_target="tpu_custom_call" | custom-call | flops 32999999488 | bytes 9900000 | tf_op jit(solution)/shard_map/quads/pallas_call | solution.py:279
  61.8 9.7 %quads.3 = (bf16[864,256]{1,0:T(8,128)(2,1)S(1)}, bf16[3,864,256]{2,1,0:T(8,128)(2,1)S(1)}, bf16[512,768]{1,0:T(8,128)(2,1)S(1)}, bf16[512,768]{1,0:T(8,128)(2,1)S(1)}) custom-call(s32[1]{0:T(128)} %bitcast.pole_ref, bf16[864,1024]{1,0:T(8,128)(2,1)S(1)} %get-tuple-element.46.n_ref, bf16[1024,864]{1,0:T(8,128)(2,1)S(1)} %get-tuple-element.47.nt_ref, ...), custom_call_target="tpu_custom_call" | custom-call | flops 11000000512 | bytes 3300000 | tf_op jit(solution)/shard_map/quads/pallas_call | solution.py:279
  71.5 3.4 %out_grads.1 = (bf16[512,1024]{1,0:T(8,128)(2,1)S(1)}, bf16[512,1024]{1,0:T(8,128)(2,1)S(1)}) custom-call(s32[128]{0:T(128)S(1)} %fusion.2.place_ref, bf16[864,768]{1,0:T(8,128)(2,1)S(1)} %get-tuple-element.49.before_ref.att_ref, bf16[864,256]{1,0:T(8,128)(2,1)S(1)} %get-tuple-element.58.after_ref.att2_ref, bf16[864,1024]{1,0:T(8,128)(2,1)S(1)} %get-tuple-element.48.gw_ref), custom_call_target="tpu_custom_call" | custom-call | flops 7000000000 | bytes 2100000 | tf_op jit(solution)/shard_map/out_grads/pallas_call | solution.py:304
  74.9 0.1 collective-permute-start.5
  75.0 0.5 collective-permute-start.4
  75.5 3.3 %collective-permute-done.4.refs_3_ = bf16[512,768]{1,0:T(8,128)(2,1)S(1)} collective-permute-done((bf16[512,768]{1,0:T(8,128)(2,1)S(1)}, bf16[512,768]{1,0:T(8,128)(2,1)S(1)}, u32[]{:S(2)}, u32[]{:S(2)}) %collective-permute-start.4) | collective-permute-done | bytes 786464 | tf_op jit(solution)/shard_map/ppermute | solution.py:54
  78.8 0.9 core_sum.1
  79.8 0.1 collective-permute-start.9
  79.8 8.5 %collective-permute-start.10 = (bf16[128,4096]{1,0:T(8,128)(2,1)S(1)}, bf16[128,4096]{1,0:T(8,128)(2,1)S(1)}, u32[]{:S(2)}, u32[]{:S(2)}) collective-permute-start(bf16[128,4096]{1,0:T(8,128)(2,1)S(1)} %get-tuple-element.70), channel_id=1, source_target_pairs={{0,6},{1,49},{2,0},{3,51},{4,2},{5,53},{6,4},{7,55},{8,14},{9,57},... | collective-permute-start | bytes 3145736 | tf_op jit(solution)/shard_map/ppermute | solution.py:82
  88.3 1.4 collective-permute-start.11
  89.7 13.5 %epilogue.1 = (bf16[2,18,24,1024]{3,2,1,0:T(8,128)(2,1)S(1)}, bf16[2,18,24,1024]{3,2,1,0:T(8,128)(2,1)S(1)}, bf16[3,144,1024]{2,1,0:T(8,128)(2,1)S(1)}, bf16[288...) custom-call(bf16[864,768]{1,0:T(8,128)(2,1)S(1)} %copy-done.9, bf16[864,256]{1,0:T(8,128)(2,1)S(1)} %get-tuple-element.58.after_ref.att2_ref, ...), custom_call_target="tpu_custom_call" | custom-call | flops 16000000000 | bytes 4800000 | tf_op jit(solution)/shard_map/epilogue/pallas_call | solution.py:358
  103.3 0.1 collective-permute-start.6
  103.3 0.3 collective-permute-start.7
  103.7 8.2 %collective-permute-done.10.refs_2_ = bf16[128,4096]{1,0:T(8,128)(2,1)S(1)} collective-permute-done((bf16[128,4096]{1,0:T(8,128)(2,1)S(1)}, bf16[128,4096]{1,0:T(8,128)(2,1)S(1)}, u32[]{:S(2)}, u32[]{:S(2)}) %collective-permute-start.10) | collective-permute-done | bytes 1048608 | tf_op jit(solution)/shard_map/ppermute | solution.py:82
  111.9 9.2 %collective-permute-done.11.refs_3_ = bf16[128,4096]{1,0:T(8,128)(2,1)S(1)} collective-permute-done((bf16[128,4096]{1,0:T(8,128)(2,1)S(1)}, bf16[128,4096]{1,0:T(8,128)(2,1)S(1)}, u32[]{:S(2)}, u32[]{:S(2)}) %collective-permute-start.11) | collective-permute-done | bytes 1048608 | tf_op jit(solution)/shard_map/ppermute | solution.py:82
  121.1 0.5 ring_sum.2
  121.6 0.1 collective-permute-start.12
  121.7 3.8 %collective-permute-start.13 = (bf16[32,4096]{1,0:T(8,128)(2,1)S(1)}, bf16[32,4096]{1,0:T(8,128)(2,1)S(1)}, u32[]{:S(2)}, u32[]{:S(2)}) collective-permute-start(bf16[32,4096]{1,0:T(8,128)(2,1)S(1)} %get-tuple-element.74), channel_id=1, source_target_pairs={{0,48},{1,7},{2,50},{3,1},{4,52},{5,3},{6,54},{7,5},{8,56},{9,15},... | collective-permute-start | bytes 786440 | tf_op jit(solution)/shard_map/ppermute | solution.py:82
  125.5 1.4 collective-permute-start.14
  126.9 3.9 %collective-permute-done.12.refs_1_ = bf16[32,4096]{1,0:T(8,128)(2,1)S(1)} collective-permute-done((bf16[32,4096]{1,0:T(8,128)(2,1)S(1)}, bf16[32,4096]{1,0:T(8,128)(2,1)S(1)}, u32[]{:S(2)}, u32[]{:S(2)}) %collective-permute-start.12) | collective-permute-done | bytes 262176 | tf_op jit(solution)/shard_map/ppermute | solution.py:82
  130.8 1.4 collective-permute-done.13.refs_2_
  132.2 1.8 %collective-permute-done.14.refs_3_ = bf16[32,4096]{1,0:T(8,128)(2,1)S(1)} collective-permute-done((bf16[32,4096]{1,0:T(8,128)(2,1)S(1)}, bf16[32,4096]{1,0:T(8,128)(2,1)S(1)}, u32[]{:S(2)}, u32[]{:S(2)}) %collective-permute-start.14) | collective-permute-done | bytes 262176 | tf_op jit(solution)/shard_map/ppermute | solution.py:82
  134.0 0.1 ring_sum.3
  134.1 1.3 collective-permute-start.15
  135.4 3.6 %collective-permute-start.16 = (f32[8,4096]{1,0:T(8,128)S(1)}, f32[8,4096]{1,0:T(8,128)S(1)}, u32[]{:S(2)}, u32[]{:S(2)}) collective-permute-start(f32[8,4096]{1,0:T(8,128)S(1)} %get-tuple-element.78), channel_id=1, source_target_pairs={{0,72},{1,73},{2,74},{3,75},{4,76},{5,77},{6,78},{7,79},{8,64},{9,... | collective-permute-start | bytes 393224 | tf_op jit(solution)/shard_map/ppermute | solution.py:82
  139.0 2.1 %collective-permute-done.8.corner_ref = bf16[80,1024]{1,0:T(8,128)(2,1)S(1)} collective-permute-done((bf16[80,1024]{1,0:T(8,128)(2,1)S(1)}, bf16[80,1024]{1,0:T(8,128)(2,1)S(1)}, u32[]{:S(2)}, u32[]{:S(2)}) %collective-permute-start.8) | collective-permute-done | bytes 163872 | tf_op jit(solution)/shard_map/ppermute | solution.py:62
  141.1 7.8 %collective-permute-start.17 = (f32[8,4096]{1,0:T(8,128)S(1)}, f32[8,4096]{1,0:T(8,128)S(1)}, u32[]{:S(2)}, u32[]{:S(2)}) collective-permute-start(f32[8,4096]{1,0:T(8,128)S(1)} %get-tuple-element.79), channel_id=1, source_target_pairs={{0,8},{1,9},{2,10},{3,11},{4,12},{5,13},{6,14},{7,15},{8,0},{9,1},... | collective-permute-start | bytes 393224 | tf_op jit(solution)/shard_map/ppermute | solution.py:82
  148.9 2.4 %restore.1 = (bf16[2,18,24,1024]{3,2,1,0:T(8,128)(2,1)}, bf16[2,18,24,1024]{3,2,1,0:T(8,128)(2,1)}) custom-call(bf16[2,18,24,1024]{3,2,1,0:T(8,128)(2,1)S(1)} %get-tuple-element.62.out_ref, bf16[2,18,24,1024]{3,2,1,0:T(8,128)(2,1)S(1)} %get-tuple-element.63.grad_ref, bf16[3,144,1024]{2,1,0:T(8,128)(2,1)S(1)} %collective-permute-done.6.cols_ref, ...), custom_call_target="tpu_custom_call" | custom-call | flops 5000000000 | bytes 1500000 | tf_op jit(solution)/shard_map/restore/pallas_call | solution.py:404
  151.3 0.6 collective-permute-done.17.d
  151.8 0.7 finish.1
  (33 shorter events, 0.1 us)
Async XLA Ops:
  0.6 1.5 copy-start.1
  2.1 1.5 copy-start.3
  3.6 12.2 %copy-start.10 = (bf16[16,20736]{1,0:T(8,128)(2,1)S(1)}, bf16[16,20736]{1,0:T(8,128)(2,1)}, u32[]{:S(2)}) copy-start(bf16[16,20736]{1,0:T(8,128)(2,1)} %param.11) | copy-start | bytes 1990660
  4.9 23.1 %collective-permute-start.2 = (bf16[80,1024]{1,0:T(8,128)(2,1)}, bf16[80,1024]{1,0:T(8,128)(2,1)S(1)}, u32[]{:S(2)}, u32[]{:S(2)}) collective-permute-start(bf16[80,1024]{1,0:T(8,128)(2,1)} %get-tuple-element.45), channel_id=1, source_target_pairs={{0,127},{1,112},{2,113},{3,114},{4,115},{5,116},{6,117},{7,118},{8... | collective-permute-start | bytes 491528 | tf_op jit(solution)/shard_map/ppermute | solution.py:62
  13.1 14.9 %collective-permute-start.1 = (bf16[288,1024]{1,0:T(8,128)(2,1)}, bf16[288,1024]{1,0:T(8,128)(2,1)}, u32[]{:S(2)}, u32[]{:S(2)}) collective-permute-start(bf16[288,1024]{1,0:T(8,128)(2,1)} %get-tuple-element.44), channel_id=1, source_target_pairs={{0,112},{1,113},{2,114},{3,115},{4,116},{5,117},{6,118},{7,119},{8... | collective-permute-start | bytes 1769480 | tf_op jit(solution)/shard_map/ppermute | solution.py:62
  14.1 13.9 %collective-permute-start = (bf16[432,1024]{1,0:T(8,128)(2,1)}, bf16[432,1024]{1,0:T(8,128)(2,1)}, u32[]{:S(2)}, u32[]{:S(2)}) collective-permute-start(bf16[432,1024]{1,0:T(8,128)(2,1)} %get-tuple-element.43), channel_id=1, source_target_pairs={{0,15},{1,0},{2,1},{3,2},{4,3},{5,4},{6,5},{7,6},{8,7},{9,8},{10,9... | collective-permute-start | bytes 2654216 | tf_op jit(solution)/shard_map/ppermute | solution.py:62
  18.0 2.1 %copy-start.11 = (pred[144]{0:T(512)(128)(4,1)S(1)}, pred[144]{0:T(512)(128)(4,1)}, u32[]{:S(2)}) copy-start(pred[144]{0:T(512)(128)(4,1)} %fusion) | copy-start | bytes 436
  23.4 4.6 %copy-start.2 = (bf16[2,18,24,1024]{3,2,1,0:T(8,128)(2,1)S(1)}, bf16[2,18,24,1024]{3,2,1,0:T(8,128)(2,1)}, u32[]{:S(2)}) copy-start(bf16[2,18,24,1024]{3,2,1,0:T(8,128)(2,1)} %lat_ref.3) | copy-start | bytes 5308420
  23.4 4.6 %copy-start.5 = (f32[1024]{0:T(1024)S(1)}, f32[1024]{0:T(1024)}, u32[]{:S(2)}) copy-start(f32[1024]{0:T(1024)} %param.10) | copy-start | bytes 12292
  28.1 1.5 copy-start.4
  29.5 5.0 %copy-start = (bf16[1024,1024]{1,0:T(8,128)(2,1)S(1)}, bf16[1024,1024]{1,0:T(8,128)(2,1)}, u32[]{:S(2)}) copy-start(bf16[1024,1024]{1,0:T(8,128)(2,1)} %wo_ref.5) | copy-start | bytes 6291460
  34.5 37.0 %copy-start.6 = (bf16[864,1024]{1,0:T(8,128)(2,1)}, bf16[864,1024]{1,0:T(8,128)(2,1)S(1)}, u32[]{:S(2)}) copy-start(bf16[864,1024]{1,0:T(8,128)(2,1)S(1)} %get-tuple-element.48.gw_ref) | copy-start | bytes 5308420
  61.8 9.7 %copy-start.8 = (bf16[864,768]{1,0:T(8,128)(2,1)}, bf16[864,768]{1,0:T(8,128)(2,1)S(1)}, u32[]{:S(2)}) copy-start(bf16[864,768]{1,0:T(8,128)(2,1)S(1)} %get-tuple-element.49.before_ref.att_ref) | copy-start | bytes 3981316
  61.8 17.0 %collective-permute-start.3 = (bf16[512,2304]{1,0:T(8,128)(2,1)}, bf16[512,2304]{1,0:T(8,128)(2,1)S(1)}, u32[]{:S(2)}, u32[]{:S(2)}) collective-permute-start(bf16[512,2304]{1,0:T(8,128)(2,1)} %get-tuple-element.52), channel_id=1, source_target_pairs={{0,1},{1,0},{2,3},{3,2},{4,5},{5,4},{6,7},{7,6},{8,9},{9,8},{10,11... | collective-permute-start | bytes 7077896 | tf_op jit(solution)/shard_map/ppermute | solution.py:54
  74.9 3.9 %collective-permute-start.5 = (bf16[512,1024]{1,0:T(8,128)(2,1)S(1)}, bf16[512,1024]{1,0:T(8,128)(2,1)S(1)}, u32[]{:S(2)}, u32[]{:S(2)}) collective-permute-start(bf16[512,1024]{1,0:T(8,128)(2,1)S(1)} %get-tuple-element.56), channel_id=1, source_target_pairs={{0,1},{1,0},{2,3},{3,2},{4,5},{5,4},{6,7},{7,6},{8,9},{9,8},{10,11... | collective-permute-start | bytes 3145736 | tf_op jit(solution)/shard_map/ppermute | solution.py:54
  75.0 3.8 %collective-permute-start.4 = (bf16[512,768]{1,0:T(8,128)(2,1)S(1)}, bf16[512,768]{1,0:T(8,128)(2,1)S(1)}, u32[]{:S(2)}, u32[]{:S(2)}) collective-permute-start(bf16[512,768]{1,0:T(8,128)(2,1)S(1)} %get-tuple-element.54), channel_id=1, source_target_pairs={{0,1},{1,0},{2,3},{3,2},{4,5},{5,4},{6,7},{7,6},{8,9},{9,8},{10,11... | collective-permute-start | bytes 2359304 | tf_op jit(solution)/shard_map/ppermute | solution.py:54
  78.8 10.9 %copy-start.7 = (bf16[864,1024]{1,0:T(8,128)(2,1)S(1)}, bf16[864,1024]{1,0:T(8,128)(2,1)}, u32[]{:S(2)}) copy-start(bf16[864,1024]{1,0:T(8,128)(2,1)} %copy-done.6) | copy-start | bytes 5308420
  78.8 10.9 %copy-start.9 = (bf16[864,768]{1,0:T(8,128)(2,1)S(1)}, bf16[864,768]{1,0:T(8,128)(2,1)}, u32[]{:S(2)}) copy-start(bf16[864,768]{1,0:T(8,128)(2,1)} %copy-done.8) | copy-start | bytes 3981316
  79.8 41.3 %collective-permute-start.9 = (bf16[128,4096]{1,0:T(8,128)(2,1)S(1)}, bf16[128,4096]{1,0:T(8,128)(2,1)S(1)}, u32[]{:S(2)}, u32[]{:S(2)}) collective-permute-start(bf16[128,4096]{1,0:T(8,128)(2,1)S(1)} %get-tuple-element.57), channel_id=1, source_target_pairs={{0,2},{1,17},{2,4},{3,19},{4,6},{5,21},{6,0},{7,23},{8,10},{9,25},... | collective-permute-start | bytes 3145736 | tf_op jit(solution)/shard_map/ppermute | solution.py:82
  79.8 32.1 %collective-permute-start.10 = (bf16[128,4096]{1,0:T(8,128)(2,1)S(1)}, bf16[128,4096]{1,0:T(8,128)(2,1)S(1)}, u32[]{:S(2)}, u32[]{:S(2)}) collective-permute-start(bf16[128,4096]{1,0:T(8,128)(2,1)S(1)} %get-tuple-element.70), channel_id=1, source_target_pairs={{0,6},{1,49},{2,0},{3,51},{4,2},{5,53},{6,4},{7,55},{8,14},{9,57},... | collective-permute-start | bytes 3145736 | tf_op jit(solution)/shard_map/ppermute | solution.py:82
  88.3 32.7 %collective-permute-start.11 = (bf16[128,4096]{1,0:T(8,128)(2,1)S(1)}, bf16[128,4096]{1,0:T(8,128)(2,1)S(1)}, u32[]{:S(2)}, u32[]{:S(2)}) collective-permute-start(bf16[128,4096]{1,0:T(8,128)(2,1)S(1)} %get-tuple-element.71), channel_id=1, source_target_pairs={{0,4},{1,33},{2,6},{3,35},{4,0},{5,37},{6,2},{7,39},{8,12},{9,41},... | collective-permute-start | bytes 3145736 | tf_op jit(solution)/shard_map/ppermute | solution.py:82
  103.3 45.6 %collective-permute-start.6 = (bf16[3,144,1024]{2,1,0:T(8,128)(2,1)S(1)}, bf16[3,144,1024]{2,1,0:T(8,128)(2,1)S(1)}, u32[]{:S(2)}, u32[]{:S(2)}) collective-permute-start(bf16[3,144,1024]{2,1,0:T(8,128)(2,1)S(1)} %get-tuple-element.64), channel_id=1, source_target_pairs={{0,1},{1,2},{2,3},{3,4},{4,5},{5,6},{6,7},{7,8},{8,9},{9,10},{10,1... | collective-permute-start | bytes 2654216 | tf_op jit(solution)/shard_map/ppermute | solution.py:62
  103.3 45.5 %collective-permute-start.7 = (bf16[288,1024]{1,0:T(8,128)(2,1)S(1)}, bf16[288,1024]{1,0:T(8,128)(2,1)S(1)}, u32[]{:S(2)}, u32[]{:S(2)}) collective-permute-start(bf16[288,1024]{1,0:T(8,128)(2,1)S(1)} %get-tuple-element.65), channel_id=1, source_target_pairs={{0,16},{1,17},{2,18},{3,19},{4,20},{5,21},{6,22},{7,23},{8,24},{9,... | collective-permute-start | bytes 1769480 | tf_op jit(solution)/shard_map/ppermute | solution.py:62
  121.6 9.2 %collective-permute-start.12 = (bf16[32,4096]{1,0:T(8,128)(2,1)S(1)}, bf16[32,4096]{1,0:T(8,128)(2,1)S(1)}, u32[]{:S(2)}, u32[]{:S(2)}) collective-permute-start(bf16[32,4096]{1,0:T(8,128)(2,1)S(1)} %get-tuple-element.73), channel_id=1, source_target_pairs={{0,16},{1,3},{2,18},{3,5},{4,20},{5,7},{6,22},{7,1},{8,24},{9,11},... | collective-permute-start | bytes 786440 | tf_op jit(solution)/shard_map/ppermute | solution.py:82
  121.7 10.6 %collective-permute-start.13 = (bf16[32,4096]{1,0:T(8,128)(2,1)S(1)}, bf16[32,4096]{1,0:T(8,128)(2,1)S(1)}, u32[]{:S(2)}, u32[]{:S(2)}) collective-permute-start(bf16[32,4096]{1,0:T(8,128)(2,1)S(1)} %get-tuple-element.74), channel_id=1, source_target_pairs={{0,48},{1,7},{2,50},{3,1},{4,52},{5,3},{6,54},{7,5},{8,56},{9,15},... | collective-permute-start | bytes 786440 | tf_op jit(solution)/shard_map/ppermute | solution.py:82
  125.5 8.5 %collective-permute-start.14 = (bf16[32,4096]{1,0:T(8,128)(2,1)S(1)}, bf16[32,4096]{1,0:T(8,128)(2,1)S(1)}, u32[]{:S(2)}, u32[]{:S(2)}) collective-permute-start(bf16[32,4096]{1,0:T(8,128)(2,1)S(1)} %get-tuple-element.75), channel_id=1, source_target_pairs={{0,32},{1,5},{2,34},{3,7},{4,36},{5,1},{6,38},{7,3},{8,40},{9,13},... | collective-permute-start | bytes 786440 | tf_op jit(solution)/shard_map/ppermute | solution.py:82
  130.8 10.3 %collective-permute-start.8 = (bf16[80,1024]{1,0:T(8,128)(2,1)S(1)}, bf16[80,1024]{1,0:T(8,128)(2,1)S(1)}, u32[]{:S(2)}, u32[]{:S(2)}) collective-permute-start(bf16[80,1024]{1,0:T(8,128)(2,1)S(1)} %get-tuple-element.66), channel_id=1, source_target_pairs={{0,17},{1,18},{2,19},{3,20},{4,21},{5,22},{6,23},{7,24},{8,25},{9,... | collective-permute-start | bytes 491528 | tf_op jit(solution)/shard_map/ppermute | solution.py:62
  134.1 17.1 %collective-permute-start.15 = (f32[8,4096]{1,0:T(8,128)S(1)}, f32[8,4096]{1,0:T(8,128)S(1)}, u32[]{:S(2)}, u32[]{:S(2)}) collective-permute-start(f32[8,4096]{1,0:T(8,128)S(1)} %get-tuple-element.77), channel_id=1, source_target_pairs={{0,64},{1,65},{2,66},{3,67},{4,68},{5,69},{6,70},{7,71},{8,72},{9,... | collective-permute-start | bytes 393224 | tf_op jit(solution)/shard_map/ppermute | solution.py:82
  135.4 15.8 %collective-permute-start.16 = (f32[8,4096]{1,0:T(8,128)S(1)}, f32[8,4096]{1,0:T(8,128)S(1)}, u32[]{:S(2)}, u32[]{:S(2)}) collective-permute-start(f32[8,4096]{1,0:T(8,128)S(1)} %get-tuple-element.78), channel_id=1, source_target_pairs={{0,72},{1,73},{2,74},{3,75},{4,76},{5,77},{6,78},{7,79},{8,64},{9,... | collective-permute-start | bytes 393224 | tf_op jit(solution)/shard_map/ppermute | solution.py:82
  141.1 10.7 %collective-permute-start.17 = (f32[8,4096]{1,0:T(8,128)S(1)}, f32[8,4096]{1,0:T(8,128)S(1)}, u32[]{:S(2)}, u32[]{:S(2)}) collective-permute-start(f32[8,4096]{1,0:T(8,128)S(1)} %get-tuple-element.79), channel_id=1, source_target_pairs={{0,8},{1,9},{2,10},{3,11},{4,12},{5,13},{6,14},{7,15},{8,0},{9,1},... | collective-permute-start | bytes 393224 | tf_op jit(solution)/shard_map/ppermute | solution.py:82
